TPU v7x, 32 devices: a whole 2x2x4 slice. The times are simulated.
32 devices in a mesh: row: 4 (over z_hi, core), col: 4 (over y, x), seq: 2 (over z_lo).
Axes of the slice: x: 2, y: 2, z: 4 (z_hi: 2, z_lo: 2; z = z_hi * 2 + z_lo), core: 2. Of those that a mesh axis runs over, the one named last changes fastest.
Arguments:
- alignment: bfloat16 [64, 128, 256], P('seq', ('row', 'col')), may hold values from -6 to 6
- left_weight: bfloat16 [256, 32], replicated, may hold values from -0.375 to 0.375
- right_weight: bfloat16 [256, 32], replicated, may hold values from -0.375 to 0.375
- out_weight: bfloat16 [1024, 128], replicated, may hold values from -0.1875 to 0.1875
- out_bias: float32 [128], replicated, may hold values from -3 to 3
- cotangent: bfloat16 [128, 128, 128], P(('row', 'seq'), 'col'), may hold values from -6 to 6
Outputs:
- pair_update: bfloat16 [128, 128, 128], P(('row', 'seq'), 'col')
- alignment_grad: float32 [64, 128, 256], P('seq', ('row', 'col'))
- left_weight_grad: float32 [256, 32], replicated
- right_weight_grad: float32 [256, 32], replicated
- out_weight_grad: float32 [1024, 128], replicated
All inputs are finite; a program needn't handle non-finite values.
Results may differ from a plain program's by a relative error of at most 0.02.
Values may be sent and summed in bfloat16 or wider, within the bound.
A program may use at most 64 MiB of HBM per device.

v0:
```python
import math

import jax
import jax.numpy as jnp
from jax import lax
from jax.sharding import PartitionSpec as P


def body(alignment, left_weight, right_weight, out_weight, out_bias, cotangent):
    proj_width = left_weight.shape[1]
    pair_width = out_weight.shape[1]
    values = alignment.astype(jnp.float32)
    center = values - jnp.mean(values, axis=2, keepdims=True)
    invstd = lax.rsqrt(jnp.mean(center * center, axis=2, keepdims=True) + 1e-05)
    scaled = center * invstd
    normed = scaled.astype(jnp.bfloat16)
    both_weights = jnp.concatenate([left_weight, right_weight], axis=1)
    projected = jnp.einsum(
        "srk,kc->src", normed, both_weights, preferred_element_type=jnp.float32
    ).astype(jnp.bfloat16)
    slab = lax.all_gather(projected, "col", axis=1, tiled=True)
    left_rows = lax.all_to_all(
        slab[:, :, :proj_width], "seq", split_axis=1, concat_axis=0, tiled=True
    )
    ratio = lax.axis_size("col") // lax.axis_size("row")
    col_index = lax.axis_index("col")
    slab_len = slab.shape[1]
    col_width = slab_len // ratio
    every_col = lax.all_gather(projected[:, :, proj_width:], ("row", "col"), axis=1, tiled=True)
    own_cols = lax.dynamic_slice_in_dim(every_col, col_index * col_width, col_width, 1)
    right_cols = lax.all_gather(own_cols, "seq", axis=0, tiled=True)
    seq_total = right_cols.shape[0]
    inverse = 1.0 / seq_total
    row_count = left_rows.shape[1]
    block_rows = math.gcd(8, row_count)
    block_count = row_count // block_rows
    left_blocks = left_rows.reshape(seq_total, block_count, block_rows, proj_width).transpose(
        1, 0, 2, 3
    )
    cot_blocks = cotangent.reshape(block_count, block_rows * col_width, pair_width)

    def one_block(carry, inputs):
        wout_total, right_total = carry
        left_piece, cot_flat = inputs
        outer = (
            jnp.einsum("sic,sjd->ijcd", left_piece, right_cols, preferred_element_type=jnp.float32)
            * inverse
        )
        outer_flat = outer.astype(jnp.bfloat16).reshape(
            block_rows * col_width, proj_width * proj_width
        )
        pair = (
            jnp.dot(outer_flat, out_weight, preferred_element_type=jnp.float32) + out_bias
        ).astype(jnp.bfloat16)
        wout_total = wout_total + lax.dot_general(
            outer_flat, cot_flat, (((0,), (0,)), ((), ())), preferred_element_type=jnp.float32
        )
        outer_grad = (
            jnp.dot(cot_flat, out_weight.T, preferred_element_type=jnp.float32) * inverse
        ).astype(jnp.bfloat16)
        outer_grad = outer_grad.reshape(block_rows, col_width, proj_width, proj_width)
        left_part = jnp.einsum(
            "ijcd,sjd->sic", outer_grad, right_cols, preferred_element_type=jnp.float32
        )
        right_total = right_total + jnp.einsum(
            "ijcd,sic->sjd", outer_grad, left_piece, preferred_element_type=jnp.float32
        )
        return (
            (wout_total, right_total),
            (pair.reshape(block_rows, col_width, pair_width), left_part),
        )

    init = (
        jnp.zeros((proj_width * proj_width, pair_width), jnp.float32),
        jnp.zeros((seq_total, col_width, proj_width), jnp.float32),
    )
    (wout_part, right_part), (pairs, left_parts) = lax.scan(
        one_block, init, (left_blocks, cot_blocks)
    )
    pair_update = pairs.reshape(row_count, col_width, pair_width)
    left_grad = left_parts.transpose(1, 0, 2, 3).reshape(seq_total, row_count, proj_width)
    left_back = lax.all_to_all(
        left_grad.astype(jnp.bfloat16), "seq", split_axis=0, concat_axis=1, tiled=True
    ).astype(left_grad.dtype)
    right_seq = lax.psum_scatter(
        right_part.astype(jnp.bfloat16), "seq", scatter_dimension=0, tiled=True
    ).astype(jnp.float32)
    left_local = lax.psum_scatter(
        left_back.astype(jnp.bfloat16), "col", scatter_dimension=1, tiled=True
    ).astype(jnp.float32)
    spread = jnp.zeros(
        (right_seq.shape[0], slab_len * lax.axis_size("row"), proj_width), jnp.float32
    )
    spread = lax.dynamic_update_slice_in_dim(spread, right_seq, col_index * col_width, 1)
    right_local = lax.psum_scatter(spread, ("row", "col"), scatter_dimension=1, tiled=True)
    grads_both = jnp.concatenate([left_local, right_local], axis=2).astype(jnp.bfloat16)
    weight_part = jnp.einsum("srk,src->kc", normed, grads_both, preferred_element_type=jnp.float32)
    normed_grad = jnp.einsum(
        "src,kc->srk", grads_both, both_weights, preferred_element_type=jnp.float32
    )
    mean_grad = jnp.mean(normed_grad, axis=2, keepdims=True)
    mean_cross = jnp.mean(normed_grad * scaled, axis=2, keepdims=True)
    alignment_grad = invstd * (normed_grad - mean_grad - scaled * mean_cross)
    weight_total, wout_total = lax.psum((weight_part, wout_part), ("row", "col", "seq"))
    residue_total = alignment.shape[1] * lax.axis_size("row") * lax.axis_size("col")
    left_weight_grad = weight_total[:, :proj_width] / residue_total
    right_weight_grad = weight_total[:, proj_width:] / residue_total
    return (
        pair_update,
        alignment_grad,
        left_weight_grad,
        right_weight_grad,
        wout_total / residue_total,
    )


def solution(mesh):
    placed = (P("seq", ("row", "col"), None), P(), P(), P(), P(), P(("row", "seq"), "col", None))
    return jax.shard_map(
        body,
        mesh=mesh,
        in_specs=placed,
        out_specs=(P(("row", "seq"), "col", None), P("seq", ("row", "col"), None), P(), P(), P()),
        check_vma=False,
    )
```

profile of v0, /device:TPU:1, one launch (start us, length us, event | category | flops | bytes accessed | tf_op | source)
XLA Modules:
  0.0 319.9 jit_solution(4549267747742743008)
XLA Ops:
  8.0 1.0 convert_reduce_fusion
  9.0 1.1 fusion.27
  10.1 0.6 copy-done.4
  10.7 1.2 convolution_convert_fusion
  11.9 7.8 %all_gather.9 = bf16[32,32,64]{2,1,0:T(8,128)(2,1)S(1)} all-gather(bf16[32,8,64]{2,1,0:T(8,128)(2,1)S(1)} %convolution_convert_fusion), channel_id=1, replica_groups=mesh['row'=4,'col'=4,'seq'=2] {'col'}, dimensions={1}, use_global_device_ids=true | all-gather | bytes 163840 | tf_op jit(solution)/shard_map/all_gather | solution.py:21
  19.8 0.9 reshape.67
  20.7 3.3 %all-to-all-start = ((bf16[2,2,8192]{2,1,0:T(2,128)(2,1)}), bf16[2,2,8192]{2,1,0:T(2,128)(2,1)S(1)}, u32[]{:S(2)}, u32[]{:S(2)}) async-start(bf16[2,2,8192]{2,1,0:T(2,128)(2,1)} %reshape.67), calls=%async_computation | async-start | bytes 131072 | tf_op jit(solution)/shard_map/all_to_all | solution.py:22
  24.2 39.9 %all_gather.10 = bf16[32,128,32]{2,1,0:T(8,128)(2,1)S(1)} all-gather(bf16[32,8,32]{2,1,0:T(8,128)(2,1)S(1)} %slice.17), channel_id=1, replica_groups=mesh['row'=4,'col'=4,'seq'=2] {'row','col'}, dimensions={1}, use_global_device_ids=true | all-gather | bytes 278528 | tf_op jit(solution)/shard_map/all_gather | solution.py:29
  64.1 6.9 %all_gather.11 = bf16[64,32,32]{2,1,0:T(8,128)(2,1)S(1)} all-gather(bf16[32,32,32]{2,1,0:T(8,128)(2,1)S(1)} %constant_dynamic-slice_fusion.1), channel_id=1, replica_groups=mesh['row'=4,'col'=4,'seq'=2] {'seq'}, dimensions={0}, use_global_device_ids=true | all-gather | bytes 196608 | tf_op jit(solution)/shard_map/all_gather | solution.py:31
  71.0 1.3 copy.54
  72.9 25.2 %while.17 = (s32[]{:T(128)}, f32[1024,128]{1,0:T(8,128)}, f32[64,32,32]{0,2,1:T(8,128)S(1)}, bf16[2,8,32,128]{3,2,1,0:T(8,128)(2,1)}, bf16[2,64,8,32]{1,3,2,0:T(...) while((s32[]{:T(128)}, f32[1024,128]{1,0:T(8,128)}, ...), condition=%wide.region_3.4_spmd.clone, body=%wide.region_2.3_spmd.clone.sunk | while | flops 303497216 | bytes 11797236 | solution.py:77
  72.9 1.1 fusion.71
  74.0 1.6 reshape.74
  75.6 2.1 fusion.74
  77.7 0.8 fusion.72
  78.7 0.7 fusion.70
  79.4 2.2 reshape.73
  81.7 1.0 fusion.73
  82.6 2.0 convolution_add_fusion.3
  84.7 0.6 copy-done.7
  85.3 1.1 fusion.71
  86.5 1.6 reshape.74
  88.0 2.1 fusion.74
  90.2 0.8 fusion.72
  91.1 0.7 fusion.70
  91.9 2.2 reshape.73
  94.1 1.0 fusion.73
  95.1 2.2 convolution_add_fusion.3
  97.4 0.6 copy-done.7
  98.0 0.8 copy.69
  98.9 1.1 copy.55
  100.4 5.3 %all_to_all.33 = bf16[2,2,8192]{2,1,0:T(2,128)(2,1)S(1)} all-to-all(bf16[2,2,8192]{2,1,0:T(2,128)(2,1)S(1)} %reshape.69), channel_id=1, replica_groups=mesh['row'=4,'col'=4,'seq'=2] {'seq'}, dimensions={0} | all-to-all | bytes 131072 | tf_op jit(solution)/shard_map/all_to_all | solution.py:82
  106.2 1.1 copy.57
  107.4 2.1 reduce-scatter.8.cloned.1.call-done
  109.5 1.0 copy.70
  110.5 0.4 copy.58
  111.3 1.3 copy-done.2
  112.7 0.6 dynamic-slice
  114.0 39.9 %all-reduce.5.cloned.1.call-done = bf16[32,32,32]{2,1,0:T(8,128)(2,1)} async-done(((bf16[32,32,32]{2,1,0:T(8,128)(2,1)}), bf16[32,32,32]{2,1,0:T(8,128)(2,1)}) %all-reduce.5.cloned.1.call-update) | async-done | bytes 65552
  153.9 0.8 constant_dynamic-slice_fusion
  154.8 23.5 %reduce-scatter.6.cloned.1.call-done = f32[32,8,32]{2,1,0:T(8,128)} async-done(((f32[32,128,32]{2,1,0:T(8,128)}), f32[32,8,32]{2,1,0:T(8,128)}) %reduce-scatter.6.cloned.1.call-update) | async-done | bytes 32784 | tf_op jit(solution)/shard_map/reduce_scatter | solution.py:95
  178.3 0.9 convert.4
  179.2 0.9 convolution_bitcast_fusion.2
  180.1 0.3 fusion.34
  180.5 0.9 fusion.26
  181.4 127.8 %all-reduce.7.cloned.1.call-done = (f32[256,64]{0,1:T(8,128)}, f32[1024,128]{1,0:T(8,128)}) async-done(((f32[256,64]{0,1:T(8,128)}, f32[1024,128]{1,0:T(8,128)}), (f32[256,64]{0,1:T(8,128)}, f32[1024,128]{1,0:T(8,128)})) %all-reduce.7.cloned.1.call-update) | async-done | bytes 589840 | tf_op jit(solution)/shard_map/psum | solution.py:104
  309.2 1.4 slice_multiply_fusion
  310.6 1.9 broadcast_multiply_fusion
  (54 shorter events, 2.4 us)
Async XLA Ops:
  10.1 0.6 copy-start.4
  20.7 51.6 %all-to-all-start = ((bf16[2,2,8192]{2,1,0:T(2,128)(2,1)}), bf16[2,2,8192]{2,1,0:T(2,128)(2,1)S(1)}, u32[]{:S(2)}, u32[]{:S(2)}) async-start(bf16[2,2,8192]{2,1,0:T(2,128)(2,1)} %reshape.67), calls=%async_computation | async-start | bytes 131072 | tf_op jit(solution)/shard_map/all_to_all | solution.py:22
  24.0 85.5 %reduce-scatter.8.cloned.1.call-start = ((), (), s32[]{:S(2)}) async-start(), calls=%async_computation.5 | async-start | bytes 196608
  24.2 48.7 %copy-start = (bf16[1024,128]{1,0:T(8,128)(2,1)S(1)}, bf16[1024,128]{1,0:T(8,128)(2,1)}, u32[]{:S(2)}) copy-start(bf16[1024,128]{1,0:T(8,128)(2,1)} %param.11) | copy-start | bytes 786436
  77.7 0.9 copy-start.1
  81.7 3.0 copy-start.6
  84.7 0.7 copy-start.7
  90.2 0.9 copy-start.1
  94.1 3.2 %copy-start.6 = (bf16[2,8,32,128]{3,2,1,0:T(8,128)(2,1)S(1)}, bf16[2,8,32,128]{3,2,1,0:T(8,128)(2,1)}, u32[]{:S(2)}) copy-start(bf16[2,8,32,128]{3,2,1,0:T(8,128)(2,1)} %get-tuple-element.262) | copy-start | bytes 393220 | tf_op jit(solution)/shard_map/while
  97.3 0.7 copy-start.7
  98.9 55.0 %all-reduce.5.cloned.1.call-start = ((), (), s32[]{:S(2)}) async-start(), calls=%async_computation.6 | async-start | bytes 524288
  107.3 70.9 %reduce-scatter.6.cloned.1.call-start = ((), (), s32[]{:S(2)}) async-start(), calls=%async_computation.4 | async-start | bytes 2228224 | tf_op jit(solution)/shard_map/reduce_scatter | solution.py:95
  110.9 1.8 copy-start.10
  111.2 68.0 %copy-start.3 = (bf16[32,8,256]{2,1,0:T(8,128)(2,1)S(1)}, bf16[32,8,256]{2,1,0:T(8,128)(2,1)}, u32[]{:S(2)}) copy-start(bf16[32,8,256]{2,1,0:T(8,128)(2,1)} %param.8) | copy-start | bytes 393220
  111.2 68.0 %copy-start.5 = (f32[32,8]{1,0:T(8,128)S(1)}, f32[32,8]{1,0:T(8,128)}, u32[]{:S(2)}) copy-start(f32[32,8]{1,0:T(8,128)} %copy-done.4) | copy-start | bytes 3076
  111.2 68.9 %copy-start.8 = (bf16[256,32]{0,1:T(8,128)(2,1)S(1)}, bf16[256,32]{0,1:T(8,128)(2,1)}, u32[]{:S(2)}) copy-start(bf16[256,32]{0,1:T(8,128)(2,1)} %param.10) | copy-start | bytes 49156
  111.2 68.9 %copy-start.9 = (bf16[256,32]{0,1:T(8,128)(2,1)S(1)}, bf16[256,32]{0,1:T(8,128)(2,1)}, u32[]{:S(2)}) copy-start(bf16[256,32]{0,1:T(8,128)(2,1)} %param.9) | copy-start | bytes 49156
  111.3 1.4 copy-start.2
  112.7 196.5 %all-reduce.7.cloned.1.call-start = ((), (), s32[]{:S(2)}) async-start(), calls=%async_computation.7 | async-start | bytes 1179648 | tf_op jit(solution)/shard_map/psum | solution.py:104
Sparse Core Ops, SparseCore 0:
  99.0 10.4 reduce-scatter.7
  112.8 65.4 reduce-scatter.5
Sparse Core Ops, SparseCore 1:
  107.4 46.4 all-reduce.4
  180.6 128.5 all-reduce.6
where the time goes:
time: 321 us; the launch traced here: 320 us
  waiting for transfers between devices  193 us (60%)
  blocking collectives  60 us (19%)
  local copies, waits for them, and re-layouts  21 us (7%)
  matrix products  18.2 us (6%)
  between operations  16.4 us (5%)
  other arithmetic  7.31 us (2%)
  starting transfers between devices  3.46 us (1%)
    psum x1, waiting for transfers between devices, body(): lax.psum((weight_part, wout_part), ('row', 'col', 'seq'))  128 us
    unnamed x6, waiting for transfers between devices  42.1 us
    all_gather x1, blocking collectives, body(): lax.all_gather(projected[:, :, proj_width:], ('row', 'col'), axis=1, tile...  39.9 us
    reduce_scatter x1, waiting for transfers between devices, body(): lax.psum_scatter(spread, ('row', 'col'), scatter_dimension=1, tiled=True)  23.5 us
    unnamed x25, local copies, waits for them, and re-layouts  8.04 us
    all_gather x1, blocking collectives, body(): slab = lax.all_gather(projected, 'col', axis=1, tiled=True)  7.81 us
    all_gather x1, blocking collectives, body(): right_cols = lax.all_gather(own_cols, 'seq', axis=0, tiled=True)  6.91 us
  transfers between devices with their start and end apart: 5, of which 4 were waited for; matrix products, arithmetic and copies ran while one was open for 3% of the time, Pallas kernels for 0%

commit v1 on v0

v1 whole, which is shorter than its diff:
```python
import functools

import jax
import jax.numpy as jnp
from jax import lax
from jax.experimental import pallas as pl
from jax.experimental.pallas import tpu as pltpu
from jax.sharding import PartitionSpec as P

F32 = jnp.float32
BF16 = jnp.bfloat16
MESH = pl.DeviceIdType.MESH
LANES = 128
DG = 8


def nn(a, b):
    return lax.dot_general(a, b, (((1,), (0,)), ((), ())), preferred_element_type=F32)


def nt(a, b):
    return lax.dot_general(a, b, (((1,), (1,)), ((), ())), preferred_element_type=F32)


def log2(n):
    assert n & (n - 1) == 0
    return n.bit_length() - 1


def div(x, n):
    return lax.shift_right_logical(x, jnp.int32(log2(n)))


def mod(x, n):
    return x & (n - 1)


def iota(shape, dim):
    return lax.broadcasted_iota(jnp.int32, shape, dim)


def zero_one(mask):
    return jnp.where(mask, 1.0, 0.0).astype(BF16)


def kernel(
    dims,
    align_ref,
    lw_ref,
    rw_ref,
    wout_ref,
    bias_ref,
    cot_ref,
    pair_ref,
    agrad_ref,
    wg_ref,
    wog_ref,
    s_l,
    s_r,
    l3,
    r3,
    rbd,
    og2,
    ot,
    wf,
    w2,
    s_lg,
    s_rg,
    r_lg,
    r_rg,
    s_w,
    r_w,
    g_w,
    s_v,
    r_v,
    g_v,
    sl_sem,
    rl_sem,
    sr_sem,
    rr_sem,
    slg_sem,
    rlg_sem,
    srg_sem,
    rrg_sem,
    w_sem,
    v_sem,
):
    R, C, SQ, SL, RB, CP, rows, cols = dims
    N = R * C * SQ
    I4 = LANES // SL
    GPB = RB // I4
    G = rows // I4
    NKB = rows // RB
    NB = cols // RB
    IJ = I4 * cols
    DH = CP // DG
    PW = DG * RB
    CH = DG * IJ
    KS = SQ * I4 * SL
    inverse = 1.0 / (SQ * SL)
    residues = RB * R * C

    r = lax.axis_index("row")
    c = lax.axis_index("col")
    s = lax.axis_index("seq")
    me = (r * C + c) * SQ + s

    def dev(lin):
        return (lin // (C * SQ), (lin // SQ) % C, lin % SQ)

    barrier = pltpu.get_barrier_semaphore()

    def greet(k, carry):
        pl.semaphore_signal(barrier, inc=1, device_id=dev((me + k) % N), device_id_type=MESH)
        return carry

    lax.fori_loop(1, N, greet, 0)

    values = align_ref[...].astype(F32)
    center = values - jnp.mean(values, axis=1, keepdims=True)
    invstd = lax.rsqrt(jnp.mean(center * center, axis=1, keepdims=True) + 1e-05)
    scaled = center * invstd
    normed = scaled.astype(BF16)
    M = SL * RB
    row_m, col_m = iota((M, M), 0), iota((M, M), 1)
    perm = zero_one(col_m == mod(row_m, SL) * RB + div(row_m, SL))
    normed_rs = nn(perm, normed).astype(BF16)
    eye = zero_one(iota((CP, CP), 0) == iota((CP, CP), 1))
    lw_t = nt(eye, lw_ref[...]).astype(BF16)
    left_t = nt(lw_t, normed_rs).astype(BF16)
    for h in range(GPB):
        s_l[h] = left_t[:, h * LANES : (h + 1) * LANES]
    spread = zero_one(iota((CP, CP * RB), 0) == div(iota((CP, CP * RB), 1), RB))
    rw_rep = nn(rw_ref[...], spread).astype(BF16)
    right_all = nn(normed_rs, rw_rep)
    lane_r = mod(iota((SL, CP * RB), 1), RB)
    right_own = jnp.zeros((SL, CP * RB), F32)
    for q in range(RB):
        right_own = jnp.where(lane_r == q, right_all[q * SL : (q + 1) * SL], right_own)
    s_r[...] = right_own.astype(BF16)

    pl.semaphore_wait(barrier, N - 1)

    l_tile, l_slot = c // NKB, c % NKB
    blk = r * C + c
    r_tile, r_slot = blk // NB, blk % NB

    def left_copy(cc):
        return pltpu.make_async_remote_copy(
            src_ref=s_l,
            dst_ref=l3.at[s, pl.ds(l_slot * GPB, GPB)],
            send_sem=sl_sem.at[cc],
            recv_sem=rl_sem.at[l_slot * SQ + s],
            device_id=(r, cc, l_tile),
            device_id_type=MESH,
        )

    def right_copy(t):
        return pltpu.make_async_remote_copy(
            src_ref=s_r,
            dst_ref=r3.at[r_slot, s],
            send_sem=sr_sem.at[t],
            recv_sem=rr_sem.at[r_slot * SQ + s],
            device_id=(t // SQ, r_tile, t % SQ),
            device_id_type=MESH,
        )

    l_here = l_tile == s
    r_here = r_tile == c
    my_t = r * SQ + s
    for t in range(R * SQ):
        away = jnp.logical_not(jnp.logical_and(r_here, my_t == t))

        @pl.when(away)
        def _():
            right_copy(t).start()

    for cc in range(C):
        away = jnp.logical_not(jnp.logical_and(l_here, c == cc))

        @pl.when(away)
        def _():
            left_copy(cc).start()

    @pl.when(r_here)
    def _():
        r3[r_slot, s] = s_r[...]

    @pl.when(l_here)
    def _():
        l3[s, pl.ds(l_slot * GPB, GPB)] = s_l[...]

    wf[...] = wout_ref[...].astype(F32)
    for d in range(CP):
        w2[d * CP : (d + 1) * CP, :] = wf[pl.ds(d, CP, stride=CP), :].astype(BF16)
    cot = cot_ref[...]
    for dh in range(DH):
        part = nt(w2[dh * DG * CP : (dh + 1) * DG * CP, :], cot) * inverse
        part = part.astype(BF16)
        for d in range(DG):
            for g in range(G):
                og2[g * CP : (g + 1) * CP, dh * CH + d * IJ : dh * CH + (d + 1) * IJ] = part[
                    d * CP : (d + 1) * CP, g * IJ : (g + 1) * IJ
                ]
    fr, fc = iota((NB * PW, CH), 0), iota((NB * PW, CH), 1)
    fold = zero_one(
        fr == mod(div(fc, RB), NB) * PW + div(fc, IJ) * RB + mod(fc, RB)
    )
    i_lane = mod(div(iota((SL, CH), 1), cols), I4)

    for k in range(NKB):
        for sq in range(SQ):
            away = jnp.logical_not(jnp.logical_and(s == sq, c == s * NKB + k))

            @pl.when(away)
            def _():
                pltpu.make_async_remote_copy(
                    src_ref=s_l,
                    dst_ref=l3.at[sq, pl.ds(k * GPB, GPB)],
                    send_sem=sl_sem.at[0],
                    recv_sem=rl_sem.at[k * SQ + sq],
                    device_id=dev((me + 1) % N),
                    device_id_type=MESH,
                ).wait_recv()

    for b in range(NB):
        for sq in range(SQ):
            away = jnp.logical_not(jnp.logical_and(s == sq, blk == c * NB + b))

            @pl.when(away)
            def _():
                pltpu.make_async_remote_copy(
                    src_ref=s_r,
                    dst_ref=r3.at[b, sq],
                    send_sem=sr_sem.at[0],
                    recv_sem=rr_sem.at[b * SQ + sq],
                    device_id=dev((me + 1) % N),
                    device_id_type=MESH,
                ).wait_recv()

    left = jnp.concatenate([l3[sq].reshape(G * CP, LANES) for sq in range(SQ)], axis=1)
    for dh in range(DH):
        gathered = jnp.concatenate(
            [
                jnp.concatenate(
                    [r3[b, sq][:, dh * PW : (dh + 1) * PW] for b in range(NB)], axis=1
                )
                for sq in range(SQ)
            ],
            axis=0,
        )
        wide = nn(gathered, fold)
        for sq in range(SQ):
            for i in range(I4):
                start = (sq * I4 + i) * SL
                rbd[start : start + SL, dh * CH : (dh + 1) * CH] = jnp.where(
                    i_lane == i, wide[sq * SL : (sq + 1) * SL], 0.0
                ).astype(BF16)

    eye_k = zero_one(iota((KS, KS), 0) == iota((KS, KS), 1))
    left_turned = nt(eye_k, left).astype(BF16)
    folded = []
    for dh in range(DH):
        z = nn(left_turned, og2[:, dh * CH : (dh + 1) * CH])
        picked = []
        for sq in range(SQ):
            y = z[sq * I4 * SL : (sq * I4 + 1) * SL]
            for i in range(1, I4):
                start = (sq * I4 + i) * SL
                y = jnp.where(i_lane == i, z[start : start + SL], y)
            picked.append(y)
        folded.append(nt(jnp.concatenate(picked, axis=0).astype(BF16), fold))
    for b in range(NB):
        for sq in range(SQ):
            s_rg[b, sq] = jnp.concatenate(
                [f[sq * SL : (sq + 1) * SL, b * PW : (b + 1) * PW] for f in folded], axis=1
            ).astype(BF16)
            owner = c * NB + b
            here = jnp.logical_and(s == sq, blk == owner)

            @pl.when(jnp.logical_not(here))
            def _():
                pltpu.make_async_remote_copy(
                    src_ref=s_rg.at[b, sq],
                    dst_ref=r_rg.at[my_t],
                    send_sem=srg_sem.at[b * SQ + sq],
                    recv_sem=rrg_sem.at[my_t],
                    device_id=(owner // C, owner % C, sq),
                    device_id_type=MESH,
                ).start()

            @pl.when(here)
            def _():
                r_rg[my_t] = s_rg[b, sq]

    lg = nt(og2[...], rbd[...]).astype(BF16)
    for sq in range(SQ):
        for g in range(G):
            s_lg[sq, g] = lg[g * CP : (g + 1) * CP, sq * LANES : (sq + 1) * LANES]
    for k in range(NKB):
        for sq in range(SQ):
            here = jnp.logical_and(s == sq, c == s * NKB + k)

            @pl.when(jnp.logical_not(here))
            def _():
                pltpu.make_async_remote_copy(
                    src_ref=s_lg.at[sq, pl.ds(k * GPB, GPB)],
                    dst_ref=r_lg.at[c],
                    send_sem=slg_sem.at[k * SQ + sq],
                    recv_sem=rlg_sem.at[c],
                    device_id=(r, s * NKB + k, sq),
                    device_id_type=MESH,
                ).start()

            @pl.when(here)
            def _():
                r_lg[c] = s_lg[sq, pl.ds(k * GPB, GPB)]

    for dh in range(DH):
        part = nn(left, rbd[:, dh * CH : (dh + 1) * CH]) * inverse
        part = part.astype(BF16)
        for d in range(DG):
            for g in range(G):
                start = (dh * DG + d) * CP
                ot[start : start + CP, g * IJ : (g + 1) * IJ] = part[
                    g * CP : (g + 1) * CP, d * IJ : (d + 1) * IJ
                ]

    def scatter(src, dst, sems, pieces):
        stride = N // pieces
        mine = me // stride

        def one(target):
            p = target // stride
            pltpu.make_async_remote_copy(
                src_ref=src.at[p],
                dst_ref=dst.at[(me - target + N) % N - 1],
                send_sem=sems.at[0],
                recv_sem=sems.at[1],
                device_id=dev(target),
                device_id_type=MESH,
            ).start()

        def step(q, carry):
            one(((mine + q) % pieces) * stride)
            return carry

        lax.fori_loop(1, pieces, step, 0)
        if stride > 1:

            @pl.when(me % stride != 0)
            def _():
                one(mine * stride)

    def drain(ref, sem):
        pltpu.make_async_copy(ref, ref, sem).wait()

    def drain_pieces(ref, sem, pieces):
        stride = N // pieces
        if stride == 1:
            drain(ref.at[pl.ds(0, pieces - 1)], sem)
        else:

            @pl.when(me % stride == 0)
            def _():
                drain(ref.at[pl.ds(0, pieces - 1)], sem)

            @pl.when(me % stride != 0)
            def _():
                drain(ref, sem)

    def gather(src, dst, tot, sems, pieces, count):
        stride = N // pieces
        mine = me // stride

        def run():
            drain(dst, sems.at[1])
            total = src[mine].astype(F32)
            for k in range(N - 1):
                total = total + dst[k].astype(F32)
            tot[mine] = (total * (1.0 / count)).astype(tot.dtype)

            def step(k, carry):
                pltpu.make_async_remote_copy(
                    src_ref=tot.at[mine],
                    dst_ref=tot.at[mine],
                    send_sem=sems.at[2],
                    recv_sem=sems.at[3],
                    device_id=dev((me + k) % N),
                    device_id_type=MESH,
                ).start()
                return carry

            lax.fori_loop(1, N, step, 0)

        if stride == 1:
            run()
        else:
            pl.when(me % stride == 0)(run)

    def finish(src, dst, tot, sems, pieces):
        stride = N // pieces
        drain_pieces(tot, sems.at[3], pieces)
        drain_pieces(src, sems.at[0], pieces)
        if stride == 1:
            drain(dst, sems.at[2])
        else:

            @pl.when(me % stride == 0)
            def _():
                drain(dst, sems.at[2])

    pieces_w = s_w.shape[0]
    wo = nn(ot[...], cot).astype(s_w.dtype)
    s_w[...] = wo.reshape(s_w.shape)
    scatter(s_w, r_w, w_sem, pieces_w)

    for cc in range(C):
        here = jnp.logical_and(l_here, c == cc)

        @pl.when(jnp.logical_not(here))
        def _():
            pltpu.make_async_remote_copy(
                src_ref=s_l,
                dst_ref=r_lg.at[cc],
                send_sem=slg_sem.at[0],
                recv_sem=rlg_sem.at[cc],
                device_id=dev((me + 1) % N),
                device_id_type=MESH,
            ).wait_recv()

    for t in range(R * SQ):
        here = jnp.logical_and(r_here, my_t == t)

        @pl.when(jnp.logical_not(here))
        def _():
            pltpu.make_async_remote_copy(
                src_ref=s_r,
                dst_ref=r_rg.at[t],
                send_sem=srg_sem.at[0],
                recv_sem=rrg_sem.at[t],
                device_id=dev((me + 1) % N),
                device_id_type=MESH,
            ).wait_recv()

    gl = r_lg[0].astype(F32)
    for cc in range(1, C):
        gl = gl + r_lg[cc].astype(F32)
    gl = jnp.concatenate([gl[h] for h in range(GPB)], axis=1).astype(BF16)
    gr = r_rg[0].astype(F32)
    for t in range(1, R * SQ):
        gr = gr + r_rg[t].astype(F32)
    gr = gr.astype(BF16)
    repeat = zero_one(iota((M, SL), 1) == div(iota((M, SL), 0), RB))
    gr_rows = nn(repeat, gr)
    gr_rows = jnp.where(
        mod(iota((M, CP * RB), 0), RB) == mod(iota((M, CP * RB), 1), RB), gr_rows, 0.0
    ).astype(BF16)
    gr_t = nt(spread, gr_rows).astype(BF16)
    wg = jnp.concatenate([nn(gl, normed_rs), nn(gr_t, normed)], axis=0)
    pieces_v = s_v.shape[0]
    per_row = wg.shape[1] // LANES
    for p in range(pieces_v):
        u, v = p // per_row, p % per_row
        s_v[p] = wg[u * 8 : (u + 1) * 8, v * LANES : (v + 1) * LANES]
    scatter(s_v, r_v, v_sem, pieces_v)

    gather(s_w, r_w, g_w, w_sem, pieces_w, residues)

    back = zero_one(row_m == mod(col_m, SL) * RB + div(col_m, SL))
    gl_rows = nt(back, gl).astype(BF16)
    gr_cols = nt(gr_rows, spread).astype(BF16)
    ng = nt(gl_rows, lw_ref[...]) + nt(gr_cols, rw_ref[...])
    mean_grad = jnp.mean(ng, axis=1, keepdims=True)
    mean_cross = jnp.mean(ng * scaled, axis=1, keepdims=True)
    agrad_ref[...] = invstd * (ng - mean_grad - scaled * mean_cross)

    gather(s_v, r_v, g_v, v_sem, pieces_v, residues)

    eye_z = zero_one(iota((LANES, LANES), 0) == iota((LANES, LANES), 1))
    w2_t = nt(eye_z, w2[...]).astype(BF16)
    pair_t = nn(w2_t, ot[...])
    pair_ref[...] = (pair_t.T + bias_ref[...]).astype(BF16)

    finish(s_w, r_w, g_w, w_sem, pieces_w)
    flat = g_w[...].reshape(CP * CP, g_w.shape[2]).astype(F32)
    for d in range(CP):
        wog_ref[pl.ds(d, CP, stride=CP), :] = flat[d * CP : (d + 1) * CP, :]
    finish(s_v, r_v, g_v, v_sem, pieces_v)
    for p in range(pieces_v):
        u, v = p // per_row, p % per_row
        wg_ref[u * 8 : (u + 1) * 8, v * LANES : (v + 1) * LANES] = g_v[p]

    for t in range(R * SQ):
        away = jnp.logical_not(jnp.logical_and(r_here, my_t == t))

        @pl.when(away)
        def _():
            right_copy(t).wait_send()

    for cc in range(C):
        away = jnp.logical_not(jnp.logical_and(l_here, c == cc))

        @pl.when(away)
        def _():
            left_copy(cc).wait_send()

    for b in range(NB):
        for sq in range(SQ):
            here = jnp.logical_and(s == sq, blk == c * NB + b)

            @pl.when(jnp.logical_not(here))
            def _():
                pltpu.make_async_copy(
                    s_rg.at[b, sq], s_rg.at[b, sq], srg_sem.at[b * SQ + sq]
                ).wait()

    for k in range(NKB):
        for sq in range(SQ):
            here = jnp.logical_and(s == sq, c == s * NKB + k)

            @pl.when(jnp.logical_not(here))
            def _():
                part = s_lg.at[sq, pl.ds(k * GPB, GPB)]
                pltpu.make_async_copy(part, part, slg_sem.at[k * SQ + sq]).wait()


def body(alignment, left_weight, right_weight, out_weight, out_bias, cotangent):
    R, C, SQ = lax.axis_size("row"), lax.axis_size("col"), lax.axis_size("seq")
    N = R * C * SQ
    SL, RB, CM = alignment.shape
    CP = left_weight.shape[1]
    CZ = out_weight.shape[1]
    rows, cols = cotangent.shape[0], cotangent.shape[1]
    dims = (R, C, SQ, SL, RB, CP, rows, cols)
    I4 = LANES // SL
    GPB, G, NKB, NB = RB // I4, rows // I4, rows // RB, cols // RB
    IJ, KS = I4 * cols, SQ * I4 * SL
    piece = max(16, CP * CP // N)
    pieces_w = CP * CP // piece
    pieces_v = 2 * CP * CM // (8 * LANES)
    vmem = pl.BlockSpec(memory_space=pltpu.VMEM)
    dma = pltpu.SemaphoreType.DMA
    pair, agrad, wg, wog = pl.pallas_call(
        functools.partial(kernel, dims),
        out_shape=(
            jax.ShapeDtypeStruct((rows * cols, CZ), BF16),
            jax.ShapeDtypeStruct((SL * RB, CM), F32),
            jax.ShapeDtypeStruct((2 * CP, CM), F32),
            jax.ShapeDtypeStruct((CP * CP, CZ), F32),
        ),
        in_specs=[vmem] * 6,
        out_specs=(vmem,) * 4,
        scratch_shapes=[
            pltpu.VMEM((GPB, CP, LANES), BF16),
            pltpu.VMEM((SL, CP * RB), BF16),
            pltpu.VMEM((SQ, G, CP, LANES), BF16),
            pltpu.VMEM((NB, SQ, SL, CP * RB), BF16),
            pltpu.VMEM((KS, CP * IJ), BF16),
            pltpu.VMEM((G * CP, CP * IJ), BF16),
            pltpu.VMEM((CP * CP, rows * cols), BF16),
            pltpu.VMEM((CP * CP, CZ), F32),
            pltpu.VMEM((CP * CP, CZ), BF16),
            pltpu.VMEM((SQ, G, CP, LANES), BF16),
            pltpu.VMEM((NB, SQ, SL, CP * RB), BF16),
            pltpu.VMEM((C, GPB, CP, LANES), BF16),
            pltpu.VMEM((R * SQ, SL, CP * RB), BF16),
            pltpu.VMEM((pieces_w, piece, CZ), BF16),
            pltpu.VMEM((N - 1, piece, CZ), BF16),
            pltpu.VMEM((pieces_w, piece, CZ), BF16),
            pltpu.VMEM((pieces_v, 8, LANES), F32),
            pltpu.VMEM((N - 1, 8, LANES), F32),
            pltpu.VMEM((pieces_v, 8, LANES), F32),
            dma((C,)),
            dma((NKB * SQ,)),
            dma((R * SQ,)),
            dma((NB * SQ,)),
            dma((NKB * SQ,)),
            dma((C,)),
            dma((NB * SQ,)),
            dma((R * SQ,)),
            dma((4,)),
            dma((4,)),
        ],
        compiler_params=pltpu.CompilerParams(
            collective_id=0, has_side_effects=True, vmem_limit_bytes=56 * 1024 * 1024
        ),
        name="outer_product_mean",
    )(
        alignment.reshape(SL * RB, CM),
        left_weight,
        right_weight,
        out_weight,
        out_bias.reshape(1, CZ),
        cotangent.reshape(rows * cols, CZ),
    )
    return (
        pair.reshape(rows, cols, CZ),
        agrad.reshape(SL, RB, CM),
        wg[:CP].T,
        wg[CP:].T,
        wog,
    )


def solution(mesh):
    placed = (P("seq", ("row", "col"), None), P(), P(), P(), P(), P(("row", "seq"), "col", None))
    return jax.shard_map(
        body,
        mesh=mesh,
        in_specs=placed,
        out_specs=(P(("row", "seq"), "col", None), P("seq", ("row", "col"), None), P(), P(), P()),
        check_vma=False,
    )
```

time: 321 us -> 48.9 us (0.15)
  waiting for transfers between devices: 193 us -> 0 us
  blocking collectives: 60 us -> 0 us
  Pallas kernels: 0 us -> 40.3 us
  matrix products: 18.2 us -> 0 us
  between operations: 16.4 us -> 0.66 us
  local copies, waits for them, and re-layouts: 21 us -> 7.69 us
  other arithmetic: 7.31 us -> 0 us
  starting transfers between devices: 3.46 us -> 0 us
    psum x1 -> x0, waiting for transfers between devices: 128 us -> none  [body(): lax.psum((weight_part, wout_part), ('row', 'col', 'seq'))]
    all_gather x3 -> x0, blocking collectives: 54.6 us -> none  [the longest x1 39.9 us: body(): lax.all_gather(projected[:, :, proj_width:], ('row', 'col'), axis=1, tile...]
    unnamed x6 -> x0, waiting for transfers between devices: 42.1 us -> none
    pallas_call x0 -> x1, Pallas kernels: none -> 40.3 us  [body(): pl.pallas_call(functools.partial(kernel, dims), out_shape=(jax.ShapeDtype...]
    reduce_scatter x1 -> x0, waiting for transfers between devices: 23.5 us -> none  [body(): lax.psum_scatter(spread, ('row', 'col'), scatter_dimension=1, tiled=True)]
    dot_general x15 -> x0, matrix products: 18.2 us -> none  [the longest x2 4.26 us: one_block(): jnp.einsum('ijcd,sjd->sic', outer_grad, right_cols, preferred_element_typ...]
    reshape x5 -> x0, local copies, waits for them, and re-layouts: 7.76 us -> none  [the longest x2 4.45 us: one_block(): outer.astype(jnp.bfloat16)]
    all_to_all x1 -> x0, blocking collectives: 5.35 us -> none  [body(): lax.all_to_all(left_grad.astype(jnp.bfloat16), 'seq', split_axis=0, conca...]
  transfers between devices with their start and end apart: 5 -> 0, of which waited for: 4 -> 0; matrix products, arithmetic and copies ran while one was open for 3% -> 0% of each run, Pallas kernels for 0% -> 0%
where the time goes in v1:
time: 48.9 us; the launch traced here: 48.6 us
  Pallas kernels  40.3 us (82%)
  local copies, waits for them, and re-layouts  7.69 us (16%)
  between operations  0.66 us (1%)
    pallas_call x1, Pallas kernels, body(): pl.pallas_call(functools.partial(kernel, dims), out_shape=(jax.ShapeDtype...  40.3 us
    unnamed x9, local copies, waits for them, and re-layouts  6.23 us
    transpose x1, local copies, waits for them, and re-layouts, body(): wg[CP:]  1.46 us

profile of v1, /device:TPU:1, one launch (start us, length us, event | category | flops | bytes accessed | tf_op | source)
XLA Modules:
  0.0 48.6 jit_solution(15542138070345307100)
XLA Ops:
  0.6 0.0 copy-start.1
  0.6 1.5 %copy.11.lw_ref = bf16[256,32]{1,0:T(8,128)(2,1)} copy(bf16[256,32]{0,1:T(8,128)(2,1)} %param.7) | data formatting | bytes 32768 | tf_op args[1]
  2.1 0.0 copy-done.1
  2.1 0.7 %copy.12.rw_ref = bf16[256,32]{1,0:T(8,128)(2,1)} copy(bf16[256,32]{0,1:T(8,128)(2,1)S(1)} %copy-done.1) | data formatting | bytes 32768 | tf_op args[2]
  2.8 40.3 %outer_product_mean.1 = (bf16[512,128]{1,0:T(8,128)(2,1)}, f32[256,256]{1,0:T(8,128)}, f32[64,256]{1,0:T(8,128)}, f32[1024,128]{1,0:T(8,128)}) custom-call(bf16[256,256]{1,0:T(8,128)(2,1)} %bitcast.11, bf16[256,32]{1,0:T(8,128)(2,1)} %copy.11.lw_ref, bf16[256,32]{1,0:T(8,128)(2,1)} %copy.12.rw_ref, bf16[1024,128]{1,0:T(8,128)(2,1)} %wout_ref.1, ...), custom_call_target="tpu_custom_call" | custom-call | tf_op jit(solution)/shard_map/outer_product_mean/pallas_call | solution.py:544
  43.1 0.0 copy-start
  43.1 1.5 %slice_bitcast_fusion = (f32[256,32]{0,1:T(8,128)}, f32[256,32]{0,1:T(8,128)}) fusion(f32[64,256]{1,0:T(8,128)} %get-tuple-element.11), kind=kLoop, calls=%fused_computation | loop fusion | bytes 131072 | tf_op jit(solution)/shard_map/transpose | solution.py:601
  44.6 1.6 %copy.16 = bf16[16,32,128]{2,1,0:T(8,128)(2,1)} copy(bf16[16,32,128]{2,1,0:T(8,128)(2,1)} %bitcast.10) | data formatting | bytes 262144
  46.1 1.7 %copy.17 = f32[32,8,256]{2,1,0:T(8,128)} copy(f32[32,8,256]{2,1,0:T(8,128)} %bitcast.9) | data formatting | bytes 524288
  47.8 0.0 copy-done
  47.8 0.8 %copy.18 = f32[1024,128]{1,0:T(8,128)} copy(f32[1024,128]{1,0:T(8,128)S(1)} %copy-done) | data formatting | bytes 1048576
Async XLA Ops:
  0.6 1.5 %copy-start.1 = (bf16[256,32]{0,1:T(8,128)(2,1)S(1)}, bf16[256,32]{0,1:T(8,128)(2,1)}, u32[]{:S(2)}) copy-start(bf16[256,32]{0,1:T(8,128)(2,1)} %param.8) | copy-start | bytes 49156
  43.1 4.7 %copy-start = (f32[1024,128]{1,0:T(8,128)S(1)}, f32[1024,128]{1,0:T(8,128)}, u32[]{:S(2)}) copy-start(f32[1024,128]{1,0:T(8,128)} %get-tuple-element.24) | copy-start | bytes 1572868

commit v2 on v1

--- a/solution.py
+++ b/solution.py
@@ -48,13 +48,18 @@
     align_ref,
     lw_ref,
     rw_ref,
+    wout_hbm,
+    bias_ref,
+    cot_hbm,
+    pair_hbm,
+    agrad_hbm,
+    gv_hbm,
+    gw_hbm,
     wout_ref,
-    bias_ref,
     cot_ref,
     pair_ref,
     agrad_ref,
-    wg_ref,
-    wog_ref,
+    io_sem,
     s_l,
     s_r,
     l3,
@@ -106,12 +111,24 @@
     me = (r * C + c) * SQ + s
 
     def dev(lin):
-        return (lin // (C * SQ), (lin // SQ) % C, lin % SQ)
+        return (div(lin, C * SQ), mod(div(lin, SQ), C), mod(lin, SQ))
+
+    loads = [
+        pltpu.make_async_copy(wout_hbm, wout_ref, io_sem.at[0]),
+        pltpu.make_async_copy(cot_hbm, cot_ref, io_sem.at[1]),
+    ]
+    for load in loads:
+        load.start()
+    stores = []
+
+    def store(src, dst):
+        stores.append(pltpu.make_async_copy(src, dst, io_sem.at[2 + len(stores)]))
+        stores[-1].start()
 
     barrier = pltpu.get_barrier_semaphore()
 
     def greet(k, carry):
-        pl.semaphore_signal(barrier, inc=1, device_id=dev((me + k) % N), device_id_type=MESH)
+        pl.semaphore_signal(barrier, inc=1, device_id=dev(me ^ k), device_id_type=MESH)
         return carry
 
     lax.fori_loop(1, N, greet, 0)
@@ -125,13 +142,13 @@
     row_m, col_m = iota((M, M), 0), iota((M, M), 1)
     perm = zero_one(col_m == mod(row_m, SL) * RB + div(row_m, SL))
     normed_rs = nn(perm, normed).astype(BF16)
-    eye = zero_one(iota((CP, CP), 0) == iota((CP, CP), 1))
-    lw_t = nt(eye, lw_ref[...]).astype(BF16)
-    left_t = nt(lw_t, normed_rs).astype(BF16)
+    left_t = nt(lw_ref[...], normed_rs).astype(BF16)
     for h in range(GPB):
         s_l[h] = left_t[:, h * LANES : (h + 1) * LANES]
     spread = zero_one(iota((CP, CP * RB), 0) == div(iota((CP, CP * RB), 1), RB))
-    rw_rep = nn(rw_ref[...], spread).astype(BF16)
+    CM = normed.shape[1]
+    eye_m = zero_one(iota((CM, CM), 0) == iota((CM, CM), 1))
+    rw_rep = nn(nt(eye_m, rw_ref[...]).astype(BF16), spread).astype(BF16)
     right_all = nn(normed_rs, rw_rep)
     lane_r = mod(iota((SL, CP * RB), 1), RB)
     right_own = jnp.zeros((SL, CP * RB), F32)
@@ -190,10 +207,14 @@
     def _():
         l3[s, pl.ds(l_slot * GPB, GPB)] = s_l[...]
 
+    for load in loads:
+        load.wait()
     wf[...] = wout_ref[...].astype(F32)
     for d in range(CP):
         w2[d * CP : (d + 1) * CP, :] = wf[pl.ds(d, CP, stride=CP), :].astype(BF16)
     cot = cot_ref[...]
+    eye_z = zero_one(iota((LANES, LANES), 0) == iota((LANES, LANES), 1))
+    w2_t = nt(eye_z, w2[...]).astype(BF16)
     for dh in range(DH):
         part = nt(w2[dh * DG * CP : (dh + 1) * DG * CP, :], cot) * inverse
         part = part.astype(BF16)
@@ -219,7 +240,7 @@
                     dst_ref=l3.at[sq, pl.ds(k * GPB, GPB)],
                     send_sem=sl_sem.at[0],
                     recv_sem=rl_sem.at[k * SQ + sq],
-                    device_id=dev((me + 1) % N),
+                    device_id=dev(me ^ 1),
                     device_id_type=MESH,
                 ).wait_recv()
 
@@ -234,7 +255,7 @@
                     dst_ref=r3.at[b, sq],
                     send_sem=sr_sem.at[0],
                     recv_sem=rr_sem.at[b * SQ + sq],
-                    device_id=dev((me + 1) % N),
+                    device_id=dev(me ^ 1),
                     device_id_type=MESH,
                 ).wait_recv()
 
@@ -257,65 +278,6 @@
                     i_lane == i, wide[sq * SL : (sq + 1) * SL], 0.0
                 ).astype(BF16)
 
-    eye_k = zero_one(iota((KS, KS), 0) == iota((KS, KS), 1))
-    left_turned = nt(eye_k, left).astype(BF16)
-    folded = []
-    for dh in range(DH):
-        z = nn(left_turned, og2[:, dh * CH : (dh + 1) * CH])
-        picked = []
-        for sq in range(SQ):
-            y = z[sq * I4 * SL : (sq * I4 + 1) * SL]
-            for i in range(1, I4):
-                start = (sq * I4 + i) * SL
-                y = jnp.where(i_lane == i, z[start : start + SL], y)
-            picked.append(y)
-        folded.append(nt(jnp.concatenate(picked, axis=0).astype(BF16), fold))
-    for b in range(NB):
-        for sq in range(SQ):
-            s_rg[b, sq] = jnp.concatenate(
-                [f[sq * SL : (sq + 1) * SL, b * PW : (b + 1) * PW] for f in folded], axis=1
-            ).astype(BF16)
-            owner = c * NB + b
-            here = jnp.logical_and(s == sq, blk == owner)
-
-            @pl.when(jnp.logical_not(here))
-            def _():
-                pltpu.make_async_remote_copy(
-                    src_ref=s_rg.at[b, sq],
-                    dst_ref=r_rg.at[my_t],
-                    send_sem=srg_sem.at[b * SQ + sq],
-                    recv_sem=rrg_sem.at[my_t],
-                    device_id=(owner // C, owner % C, sq),
-                    device_id_type=MESH,
-                ).start()
-
-            @pl.when(here)
-            def _():
-                r_rg[my_t] = s_rg[b, sq]
-
-    lg = nt(og2[...], rbd[...]).astype(BF16)
-    for sq in range(SQ):
-        for g in range(G):
-            s_lg[sq, g] = lg[g * CP : (g + 1) * CP, sq * LANES : (sq + 1) * LANES]
-    for k in range(NKB):
-        for sq in range(SQ):
-            here = jnp.logical_and(s == sq, c == s * NKB + k)
-
-            @pl.when(jnp.logical_not(here))
-            def _():
-                pltpu.make_async_remote_copy(
-                    src_ref=s_lg.at[sq, pl.ds(k * GPB, GPB)],
-                    dst_ref=r_lg.at[c],
-                    send_sem=slg_sem.at[k * SQ + sq],
-                    recv_sem=rlg_sem.at[c],
-                    device_id=(r, s * NKB + k, sq),
-                    device_id_type=MESH,
-                ).start()
-
-            @pl.when(here)
-            def _():
-                r_lg[c] = s_lg[sq, pl.ds(k * GPB, GPB)]
-
     for dh in range(DH):
         part = nn(left, rbd[:, dh * CH : (dh + 1) * CH]) * inverse
         part = part.astype(BF16)
@@ -328,13 +290,13 @@
 
     def scatter(src, dst, sems, pieces):
         stride = N // pieces
-        mine = me // stride
+        mine = div(me, stride)
 
         def one(target):
-            p = target // stride
+            p = div(target, stride)
             pltpu.make_async_remote_copy(
                 src_ref=src.at[p],
-                dst_ref=dst.at[(me - target + N) % N - 1],
+                dst_ref=dst.at[(me ^ target) - 1],
                 send_sem=sems.at[0],
                 recv_sem=sems.at[1],
                 device_id=dev(target),
@@ -342,13 +304,13 @@
             ).start()
 
         def step(q, carry):
-            one(((mine + q) % pieces) * stride)
+            one((mine ^ q) * stride)
             return carry
 
         lax.fori_loop(1, pieces, step, 0)
         if stride > 1:
 
-            @pl.when(me % stride != 0)
+            @pl.when(mod(me, stride) != 0)
             def _():
                 one(mine * stride)
 
@@ -361,17 +323,17 @@
             drain(ref.at[pl.ds(0, pieces - 1)], sem)
         else:
 
-            @pl.when(me % stride == 0)
+            @pl.when(mod(me, stride) == 0)
             def _():
                 drain(ref.at[pl.ds(0, pieces - 1)], sem)
 
-            @pl.when(me % stride != 0)
+            @pl.when(mod(me, stride) != 0)
             def _():
                 drain(ref, sem)
 
     def gather(src, dst, tot, sems, pieces, count):
         stride = N // pieces
-        mine = me // stride
+        mine = div(me, stride)
 
         def run():
             drain(dst, sems.at[1])
@@ -386,7 +348,7 @@
                     dst_ref=tot.at[mine],
                     send_sem=sems.at[2],
                     recv_sem=sems.at[3],
-                    device_id=dev((me + k) % N),
+                    device_id=dev(me ^ k),
                     device_id_type=MESH,
                 ).start()
                 return carry
@@ -396,7 +358,7 @@
         if stride == 1:
             run()
         else:
-            pl.when(me % stride == 0)(run)
+            pl.when(mod(me, stride) == 0)(run)
 
     def finish(src, dst, tot, sems, pieces):
         stride = N // pieces
@@ -406,7 +368,7 @@
             drain(dst, sems.at[2])
         else:
 
-            @pl.when(me % stride == 0)
+            @pl.when(mod(me, stride) == 0)
             def _():
                 drain(dst, sems.at[2])
 
@@ -414,6 +376,69 @@
     wo = nn(ot[...], cot).astype(s_w.dtype)
     s_w[...] = wo.reshape(s_w.shape)
     scatter(s_w, r_w, w_sem, pieces_w)
+
+    eye_k = zero_one(iota((KS, KS), 0) == iota((KS, KS), 1))
+    left_turned = nt(eye_k, left).astype(BF16)
+    folded = []
+    for dh in range(DH):
+        z = nn(left_turned, og2[:, dh * CH : (dh + 1) * CH])
+        picked = []
+        for sq in range(SQ):
+            y = z[sq * I4 * SL : (sq * I4 + 1) * SL]
+            for i in range(1, I4):
+                start = (sq * I4 + i) * SL
+                y = jnp.where(i_lane == i, z[start : start + SL], y)
+            picked.append(y)
+        folded.append(nt(jnp.concatenate(picked, axis=0).astype(BF16), fold))
+    for b in range(NB):
+        for sq in range(SQ):
+            s_rg[b, sq] = jnp.concatenate(
+                [f[sq * SL : (sq + 1) * SL, b * PW : (b + 1) * PW] for f in folded], axis=1
+            ).astype(BF16)
+            owner = c * NB + b
+            here = jnp.logical_and(s == sq, blk == owner)
+
+            @pl.when(jnp.logical_not(here))
+            def _():
+                pltpu.make_async_remote_copy(
+                    src_ref=s_rg.at[b, sq],
+                    dst_ref=r_rg.at[my_t],
+                    send_sem=srg_sem.at[b * SQ + sq],
+                    recv_sem=rrg_sem.at[my_t],
+                    device_id=(owner // C, owner % C, sq),
+                    device_id_type=MESH,
+                ).start()
+
+            @pl.when(here)
+            def _():
+                r_rg[my_t] = s_rg[b, sq]
+
+    lg = nt(og2[...], rbd[...]).astype(BF16)
+    for sq in range(SQ):
+        for g in range(G):
+            s_lg[sq, g] = lg[g * CP : (g + 1) * CP, sq * LANES : (sq + 1) * LANES]
+    for k in range(NKB):
+        for sq in range(SQ):
+            here = jnp.logical_and(s == sq, c == s * NKB + k)
+
+            @pl.when(jnp.logical_not(here))
+            def _():
+                pltpu.make_async_remote_copy(
+                    src_ref=s_lg.at[sq, pl.ds(k * GPB, GPB)],
+                    dst_ref=r_lg.at[c],
+                    send_sem=slg_sem.at[k * SQ + sq],
+                    recv_sem=rlg_sem.at[c],
+                    device_id=(r, s * NKB + k, sq),
+                    device_id_type=MESH,
+                ).start()
+
+            @pl.when(here)
+            def _():
+                r_lg[c] = s_lg[sq, pl.ds(k * GPB, GPB)]
+
+    pair_t = nn(w2_t, ot[...])
+    pair_ref[...] = (pair_t.T + bias_ref[...]).astype(BF16)
+    store(pair_ref, pair_hbm)
 
     for cc in range(C):
         here = jnp.logical_and(l_here, c == cc)
@@ -425,7 +450,7 @@
                 dst_ref=r_lg.at[cc],
                 send_sem=slg_sem.at[0],
                 recv_sem=rlg_sem.at[cc],
-                device_id=dev((me + 1) % N),
+                device_id=dev(me ^ 1),
                 device_id_type=MESH,
             ).wait_recv()
 
@@ -439,7 +464,7 @@
                 dst_ref=r_rg.at[t],
                 send_sem=srg_sem.at[0],
                 recv_sem=rrg_sem.at[t],
-                device_id=dev((me + 1) % N),
+                device_id=dev(me ^ 1),
                 device_id_type=MESH,
             ).wait_recv()
 
@@ -462,7 +487,7 @@
     per_row = wg.shape[1] // LANES
     for p in range(pieces_v):
         u, v = p // per_row, p % per_row
-        s_v[p] = wg[u * 8 : (u + 1) * 8, v * LANES : (v + 1) * LANES]
+        s_v[p] = wg[u * 16 : (u + 1) * 16, v * LANES : (v + 1) * LANES].astype(s_v.dtype)
     scatter(s_v, r_v, v_sem, pieces_v)
 
     gather(s_w, r_w, g_w, w_sem, pieces_w, residues)
@@ -470,26 +495,18 @@
     back = zero_one(row_m == mod(col_m, SL) * RB + div(col_m, SL))
     gl_rows = nt(back, gl).astype(BF16)
     gr_cols = nt(gr_rows, spread).astype(BF16)
-    ng = nt(gl_rows, lw_ref[...]) + nt(gr_cols, rw_ref[...])
+    ng = nn(gl_rows, lw_ref[...]) + nn(gr_cols, rw_ref[...])
     mean_grad = jnp.mean(ng, axis=1, keepdims=True)
     mean_cross = jnp.mean(ng * scaled, axis=1, keepdims=True)
     agrad_ref[...] = invstd * (ng - mean_grad - scaled * mean_cross)
+    store(agrad_ref, agrad_hbm)
 
     gather(s_v, r_v, g_v, v_sem, pieces_v, residues)
 
-    eye_z = zero_one(iota((LANES, LANES), 0) == iota((LANES, LANES), 1))
-    w2_t = nt(eye_z, w2[...]).astype(BF16)
-    pair_t = nn(w2_t, ot[...])
-    pair_ref[...] = (pair_t.T + bias_ref[...]).astype(BF16)
-
+    finish(s_v, r_v, g_v, v_sem, pieces_v)
+    store(g_v, gv_hbm)
     finish(s_w, r_w, g_w, w_sem, pieces_w)
-    flat = g_w[...].reshape(CP * CP, g_w.shape[2]).astype(F32)
-    for d in range(CP):
-        wog_ref[pl.ds(d, CP, stride=CP), :] = flat[d * CP : (d + 1) * CP, :]
-    finish(s_v, r_v, g_v, v_sem, pieces_v)
-    for p in range(pieces_v):
-        u, v = p // per_row, p % per_row
-        wg_ref[u * 8 : (u + 1) * 8, v * LANES : (v + 1) * LANES] = g_v[p]
+    store(g_w, gw_hbm)
 
     for t in range(R * SQ):
         away = jnp.logical_not(jnp.logical_and(r_here, my_t == t))
@@ -523,6 +540,30 @@
             def _():
                 part = s_lg.at[sq, pl.ds(k * GPB, GPB)]
                 pltpu.make_async_copy(part, part, slg_sem.at[k * SQ + sq]).wait()
+
+    for copy in stores:
+        copy.wait()
+
+
+def finishing(pair_in, agrad_in, gv_ref, gw_ref, pair_out, agrad_out, lwg, rwg, wog, sems):
+    copies = [
+        pltpu.make_async_copy(pair_in, pair_out, sems.at[0]),
+        pltpu.make_async_copy(agrad_in, agrad_out, sems.at[1]),
+    ]
+    for copy in copies:
+        copy.start()
+    pieces, piece, CZ = gw_ref.shape
+    CP = lwg.shape[0]
+    flat = gw_ref[...].reshape(CP * CP, CZ).astype(F32)
+    for d in range(CP):
+        wog[pl.ds(d, CP, stride=CP), :] = flat[d * CP : (d + 1) * CP, :]
+    per_row = lwg.shape[1] // LANES
+    for p in range(gv_ref.shape[0]):
+        u, v = p // per_row, p % per_row
+        out, start = (lwg, u * 16) if u * 16 < CP else (rwg, u * 16 - CP)
+        out[start : start + 16, v * LANES : (v + 1) * LANES] = gv_ref[p].astype(F32)
+    for copy in copies:
+        copy.wait()
 
 
 def body(alignment, left_weight, right_weight, out_weight, out_bias, cotangent):
@@ -538,20 +579,26 @@
     IJ, KS = I4 * cols, SQ * I4 * SL
     piece = max(16, CP * CP // N)
     pieces_w = CP * CP // piece
-    pieces_v = 2 * CP * CM // (8 * LANES)
+    pieces_v = 2 * CP * CM // (16 * LANES)
     vmem = pl.BlockSpec(memory_space=pltpu.VMEM)
     dma = pltpu.SemaphoreType.DMA
-    pair, agrad, wg, wog = pl.pallas_call(
+    hbm = pl.BlockSpec(memory_space=pl.ANY)
+    pair, agrad, gv, gw = pl.pallas_call(
         functools.partial(kernel, dims),
         out_shape=(
             jax.ShapeDtypeStruct((rows * cols, CZ), BF16),
             jax.ShapeDtypeStruct((SL * RB, CM), F32),
-            jax.ShapeDtypeStruct((2 * CP, CM), F32),
-            jax.ShapeDtypeStruct((CP * CP, CZ), F32),
+            jax.ShapeDtypeStruct((pieces_v, 16, LANES), BF16),
+            jax.ShapeDtypeStruct((pieces_w, piece, CZ), BF16),
         ),
-        in_specs=[vmem] * 6,
-        out_specs=(vmem,) * 4,
+        in_specs=[vmem, vmem, vmem, hbm, vmem, hbm],
+        out_specs=(hbm,) * 4,
         scratch_shapes=[
+            pltpu.VMEM((CP * CP, CZ), BF16),
+            pltpu.VMEM((rows * cols, CZ), BF16),
+            pltpu.VMEM((rows * cols, CZ), BF16),
+            pltpu.VMEM((SL * RB, CM), F32),
+            dma((6,)),
             pltpu.VMEM((GPB, CP, LANES), BF16),
             pltpu.VMEM((SL, CP * RB), BF16),
             pltpu.VMEM((SQ, G, CP, LANES), BF16),
@@ -568,9 +615,9 @@
             pltpu.VMEM((pieces_w, piece, CZ), BF16),
             pltpu.VMEM((N - 1, piece, CZ), BF16),
             pltpu.VMEM((pieces_w, piece, CZ), BF16),
-            pltpu.VMEM((pieces_v, 8, LANES), F32),
-            pltpu.VMEM((N - 1, 8, LANES), F32),
-            pltpu.VMEM((pieces_v, 8, LANES), F32),
+            pltpu.VMEM((pieces_v, 16, LANES), BF16),
+            pltpu.VMEM((N - 1, 16, LANES), BF16),
+            pltpu.VMEM((pieces_v, 16, LANES), BF16),
             dma((C,)),
             dma((NKB * SQ,)),
             dma((R * SQ,)),
@@ -588,17 +635,32 @@
         name="outer_product_mean",
     )(
         alignment.reshape(SL * RB, CM),
-        left_weight,
-        right_weight,
+        left_weight.T,
+        right_weight.T,
         out_weight,
         out_bias.reshape(1, CZ),
         cotangent.reshape(rows * cols, CZ),
     )
+    pair, agrad, lwg, rwg, wog = pl.pallas_call(
+        finishing,
+        out_shape=(
+            jax.ShapeDtypeStruct(pair.shape, BF16),
+            jax.ShapeDtypeStruct(agrad.shape, F32),
+            jax.ShapeDtypeStruct((CP, CM), F32),
+            jax.ShapeDtypeStruct((CP, CM), F32),
+            jax.ShapeDtypeStruct((CP * CP, CZ), F32),
+        ),
+        in_specs=[hbm, hbm, vmem, vmem],
+        out_specs=(hbm, hbm, vmem, vmem, vmem),
+        scratch_shapes=[dma((2,))],
+        compiler_params=pltpu.CompilerParams(vmem_limit_bytes=56 * 1024 * 1024),
+        name="finishing",
+    )(pair, agrad, gv, gw)
     return (
         pair.reshape(rows, cols, CZ),
         agrad.reshape(SL, RB, CM),
-        wg[:CP].T,
-        wg[CP:].T,
+        lwg.T,
+        rwg.T,
         wog,
     )
 

time: 48.9 us -> 55.2 us (1.13)
  the two profiles are of different devices: /device:TPU:1 before, /device:TPU:0 now
where the time goes in v2:
time: 55.2 us; the launch traced here: 55 us
  Pallas kernels  54.4 us (99%)
  between operations  0.64 us (1%)
    pallas_call x1, Pallas kernels, body(): pl.pallas_call(functools.partial(kernel, dims), out_shape=(jax.ShapeDtype...  39.5 us
    pallas_call x1, Pallas kernels, body(): pl.pallas_call(finishing, out_shape=(jax.ShapeDtypeStruct(pair.shape, BF1...  14.8 us

profile of v2, /device:TPU:0, one launch (start us, length us, event | category | flops | bytes accessed | tf_op | source)
XLA Modules:
  0.0 55.0 jit_solution(923561169123136382)
XLA Ops:
  0.6 39.5 %outer_product_mean.1 = (bf16[512,128]{1,0:T(8,128)(2,1)}, f32[256,256]{1,0:T(8,128)}, bf16[8,16,128]{2,1,0:T(8,128)(2,1)}, bf16[32,32,128]{2,1,0:T(8,128)(2,1)}) custom-call(bf16[256,256]{1,0:T(8,128)(2,1)} %bitcast.9, bf16[32,256]{1,0:T(8,128)(2,1)} %bitcast.11, bf16[32,256]{1,0:T(8,128)(2,1)} %bitcast.12, bf16[1024,128]{1,0:T(8,128)(2,1)} %wout_hbm.1, ...), custom_call_target="tpu_custom_call" | custom-call | tf_op jit(solution)/shard_map/outer_product_mean/pallas_call | solution.py:586
  40.2 14.8 %finishing.1 = (bf16[512,128]{1,0:T(8,128)(2,1)}, f32[256,256]{1,0:T(8,128)}, f32[32,256]{1,0:T(8,128)}, f32[32,256]{1,0:T(8,128)}, f32[1024,128]{1,0:T(8,128)}) custom-call(bf16[512,128]{1,0:T(8,128)(2,1)} %get-tuple-element.14.pair_in, f32[256,256]{1,0:T(8,128)} %get-tuple-element.15.agrad_in, bf16[8,16,128]{2,1,0:T(8,128)(2,1)} %get-tuple-element.16.gv_ref, ...), custom_call_target="tpu_custom_call" | custom-call | tf_op jit(solution)/shard_map/finishing/pallas_call | solution.py:644

commit v3 on v2

--- a/solution.py
+++ b/solution.py
@@ -74,11 +74,16 @@
     r_lg,
     r_rg,
     s_w,
-    r_w,
-    g_w,
+    b_w,
+    p_w,
+    q_w,
+    z_w,
+    f_w,
     s_v,
-    r_v,
-    g_v,
+    b_v,
+    p_v,
+    z_v,
+    f_v,
     sl_sem,
     rl_sem,
     sr_sem,
@@ -288,94 +293,48 @@
                     g * CP : (g + 1) * CP, d * IJ : (d + 1) * IJ
                 ]
 
-    def scatter(src, dst, sems, pieces):
-        stride = N // pieces
-        mine = div(me, stride)
-
-        def one(target):
-            p = div(target, stride)
-            pltpu.make_async_remote_copy(
-                src_ref=src.at[p],
-                dst_ref=dst.at[(me ^ target) - 1],
-                send_sem=sems.at[0],
-                recv_sem=sems.at[1],
-                device_id=dev(target),
-                device_id_type=MESH,
-            ).start()
-
-        def step(q, carry):
-            one((mine ^ q) * stride)
-            return carry
-
-        lax.fori_loop(1, pieces, step, 0)
-        if stride > 1:
-
-            @pl.when(mod(me, stride) != 0)
-            def _():
-                one(mine * stride)
+    core = mod(r, 2)
+    sibling = (r ^ 1, c, s)
+    NZ = R * SQ // 2
+    zq = div(r, 2) * SQ + s
+
+    def send(src, dst, sems, phase, target):
+        pltpu.make_async_remote_copy(
+            src_ref=src,
+            dst_ref=dst,
+            send_sem=sems.at[2 * phase],
+            recv_sem=sems.at[2 * phase + 1],
+            device_id=target,
+            device_id_type=MESH,
+        ).start()
+
+    def send_plane(src, dst, sems, phase):
+        for k in range(1, C):
+            send(src, dst, sems, phase, (r, c ^ k, s))
+
+    def send_line(ref, sems, phase):
+        for k in range(1, NZ):
+            other = zq ^ k
+            send(
+                ref.at[zq],
+                ref.at[zq],
+                sems,
+                phase,
+                (div(other, SQ) * 2 + core, c, mod(other, SQ)),
+            )
 
     def drain(ref, sem):
         pltpu.make_async_copy(ref, ref, sem).wait()
 
-    def drain_pieces(ref, sem, pieces):
-        stride = N // pieces
-        if stride == 1:
-            drain(ref.at[pl.ds(0, pieces - 1)], sem)
-        else:
-
-            @pl.when(mod(me, stride) == 0)
-            def _():
-                drain(ref.at[pl.ds(0, pieces - 1)], sem)
-
-            @pl.when(mod(me, stride) != 0)
-            def _():
-                drain(ref, sem)
-
-    def gather(src, dst, tot, sems, pieces, count):
-        stride = N // pieces
-        mine = div(me, stride)
-
-        def run():
-            drain(dst, sems.at[1])
-            total = src[mine].astype(F32)
-            for k in range(N - 1):
-                total = total + dst[k].astype(F32)
-            tot[mine] = (total * (1.0 / count)).astype(tot.dtype)
-
-            def step(k, carry):
-                pltpu.make_async_remote_copy(
-                    src_ref=tot.at[mine],
-                    dst_ref=tot.at[mine],
-                    send_sem=sems.at[2],
-                    recv_sem=sems.at[3],
-                    device_id=dev(me ^ k),
-                    device_id_type=MESH,
-                ).start()
-                return carry
-
-            lax.fori_loop(1, N, step, 0)
-
-        if stride == 1:
-            run()
-        else:
-            pl.when(mod(me, stride) == 0)(run)
-
-    def finish(src, dst, tot, sems, pieces):
-        stride = N // pieces
-        drain_pieces(tot, sems.at[3], pieces)
-        drain_pieces(src, sems.at[0], pieces)
-        if stride == 1:
-            drain(dst, sems.at[2])
-        else:
-
-            @pl.when(mod(me, stride) == 0)
-            def _():
-                drain(dst, sems.at[2])
-
-    pieces_w = s_w.shape[0]
-    wo = nn(ot[...], cot).astype(s_w.dtype)
-    s_w[...] = wo.reshape(s_w.shape)
-    scatter(s_w, r_w, w_sem, pieces_w)
+    def total(ref, count):
+        out = ref[0].astype(F32)
+        for k in range(1, count):
+            out = out + ref[k].astype(F32)
+        return out
+
+    wo = nn(ot[...], cot)
+    s_w[...] = wo.astype(BF16).reshape(s_w.shape)
+    send(s_w.at[1 - core], b_w, w_sem, 0, sibling)
 
     eye_k = zero_one(iota((KS, KS), 0) == iota((KS, KS), 1))
     left_turned = nt(eye_k, left).astype(BF16)
@@ -413,6 +372,11 @@
             def _():
                 r_rg[my_t] = s_rg[b, sq]
 
+    drain(b_w, w_sem.at[1])
+    p_w[...] = (s_w[core].astype(F32) + b_w[...].astype(F32)).astype(BF16).reshape(p_w.shape)
+    for k in range(1, C):
+        send(p_w.at[c ^ k], q_w.at[k - 1], w_sem, 1, (r, c ^ k, s))
+
     lg = nt(og2[...], rbd[...]).astype(BF16)
     for sq in range(SQ):
         for g in range(G):
@@ -439,6 +403,10 @@
     pair_t = nn(w2_t, ot[...])
     pair_ref[...] = (pair_t.T + bias_ref[...]).astype(BF16)
     store(pair_ref, pair_hbm)
+
+    drain(q_w, w_sem.at[3])
+    z_w[zq] = (p_w[c].astype(F32) + total(q_w, C - 1)).astype(BF16)
+    send_line(z_w, w_sem, 2)
 
     for cc in range(C):
         here = jnp.logical_and(l_here, c == cc)
@@ -482,15 +450,17 @@
         mod(iota((M, CP * RB), 0), RB) == mod(iota((M, CP * RB), 1), RB), gr_rows, 0.0
     ).astype(BF16)
     gr_t = nt(spread, gr_rows).astype(BF16)
-    wg = jnp.concatenate([nn(gl, normed_rs), nn(gr_t, normed)], axis=0)
-    pieces_v = s_v.shape[0]
-    per_row = wg.shape[1] // LANES
-    for p in range(pieces_v):
-        u, v = p // per_row, p % per_row
-        s_v[p] = wg[u * 16 : (u + 1) * 16, v * LANES : (v + 1) * LANES].astype(s_v.dtype)
-    scatter(s_v, r_v, v_sem, pieces_v)
-
-    gather(s_w, r_w, g_w, w_sem, pieces_w, residues)
+    s_v[0] = nn(gl, normed_rs).astype(BF16)
+    s_v[1] = nn(gr_t, normed).astype(BF16)
+    send(s_v.at[1 - core], b_v, v_sem, 0, sibling)
+
+    drain(z_w.at[pl.ds(0, NZ - 1)], w_sem.at[5])
+    f_w[core, c] = (total(z_w, NZ) * (1.0 / residues)).astype(BF16)
+    send_plane(f_w.at[core, c], f_w.at[core, c], w_sem, 3)
+
+    drain(b_v, v_sem.at[1])
+    p_v[c] = (s_v[core].astype(F32) + b_v[...].astype(F32)).astype(BF16)
+    send_plane(p_v.at[c], p_v.at[c], v_sem, 1)
 
     back = zero_one(row_m == mod(col_m, SL) * RB + div(col_m, SL))
     gl_rows = nt(back, gl).astype(BF16)
@@ -501,13 +471,31 @@
     agrad_ref[...] = invstd * (ng - mean_grad - scaled * mean_cross)
     store(agrad_ref, agrad_hbm)
 
-    gather(s_v, r_v, g_v, v_sem, pieces_v, residues)
-
-    finish(s_v, r_v, g_v, v_sem, pieces_v)
-    store(g_v, gv_hbm)
-    finish(s_w, r_w, g_w, w_sem, pieces_w)
-    store(g_w, gw_hbm)
-
+    drain(p_v.at[pl.ds(0, C - 1)], v_sem.at[3])
+    z_v[zq] = total(p_v, C).astype(BF16)
+    send_line(z_v, v_sem, 2)
+
+    drain(f_w.at[0, pl.ds(0, C - 1)], w_sem.at[7])
+    send(f_w.at[core], f_w.at[core], w_sem, 4, sibling)
+
+    drain(z_v.at[pl.ds(0, NZ - 1)], v_sem.at[5])
+    f_v[core] = (total(z_v, NZ) * (1.0 / residues)).astype(BF16)
+    send(f_v.at[core], f_v.at[core], v_sem, 3, sibling)
+
+    drain(f_w.at[0], w_sem.at[9])
+    store(f_w, gw_hbm)
+    drain(f_v.at[0], v_sem.at[7])
+    store(f_v, gv_hbm)
+
+    drain(b_w, w_sem.at[0])
+    drain(q_w, w_sem.at[2])
+    drain(z_w.at[pl.ds(0, NZ - 1)], w_sem.at[4])
+    drain(f_w.at[0, pl.ds(0, C - 1)], w_sem.at[6])
+    drain(f_w.at[0], w_sem.at[8])
+    drain(b_v, v_sem.at[0])
+    drain(p_v.at[pl.ds(0, C - 1)], v_sem.at[2])
+    drain(z_v.at[pl.ds(0, NZ - 1)], v_sem.at[4])
+    drain(f_v.at[0], v_sem.at[6])
     for t in range(R * SQ):
         away = jnp.logical_not(jnp.logical_and(r_here, my_t == t))
 
@@ -545,25 +533,15 @@
         copy.wait()
 
 
-def finishing(pair_in, agrad_in, gv_ref, gw_ref, pair_out, agrad_out, lwg, rwg, wog, sems):
-    copies = [
-        pltpu.make_async_copy(pair_in, pair_out, sems.at[0]),
-        pltpu.make_async_copy(agrad_in, agrad_out, sems.at[1]),
-    ]
-    for copy in copies:
-        copy.start()
-    pieces, piece, CZ = gw_ref.shape
+def finishing(pair_in, agrad_in, gv_ref, gw_ref, pair_out, agrad_out, lwg, rwg, wog):
+    pair_out[...] = pair_in[...]
+    agrad_out[...] = agrad_in[...]
     CP = lwg.shape[0]
-    flat = gw_ref[...].reshape(CP * CP, CZ).astype(F32)
+    flat = gw_ref[...].reshape(CP * CP, gw_ref.shape[-1]).astype(F32)
     for d in range(CP):
         wog[pl.ds(d, CP, stride=CP), :] = flat[d * CP : (d + 1) * CP, :]
-    per_row = lwg.shape[1] // LANES
-    for p in range(gv_ref.shape[0]):
-        u, v = p // per_row, p % per_row
-        out, start = (lwg, u * 16) if u * 16 < CP else (rwg, u * 16 - CP)
-        out[start : start + 16, v * LANES : (v + 1) * LANES] = gv_ref[p].astype(F32)
-    for copy in copies:
-        copy.wait()
+    lwg[...] = gv_ref[0].astype(F32)
+    rwg[...] = gv_ref[1].astype(F32)
 
 
 def body(alignment, left_weight, right_weight, out_weight, out_bias, cotangent):
@@ -577,9 +555,7 @@
     I4 = LANES // SL
     GPB, G, NKB, NB = RB // I4, rows // I4, rows // RB, cols // RB
     IJ, KS = I4 * cols, SQ * I4 * SL
-    piece = max(16, CP * CP // N)
-    pieces_w = CP * CP // piece
-    pieces_v = 2 * CP * CM // (16 * LANES)
+    H, NZ = CP * CP // 2, R * SQ // 2
     vmem = pl.BlockSpec(memory_space=pltpu.VMEM)
     dma = pltpu.SemaphoreType.DMA
     hbm = pl.BlockSpec(memory_space=pl.ANY)
@@ -588,8 +564,8 @@
         out_shape=(
             jax.ShapeDtypeStruct((rows * cols, CZ), BF16),
             jax.ShapeDtypeStruct((SL * RB, CM), F32),
-            jax.ShapeDtypeStruct((pieces_v, 16, LANES), BF16),
-            jax.ShapeDtypeStruct((pieces_w, piece, CZ), BF16),
+            jax.ShapeDtypeStruct((2, CP, CM), BF16),
+            jax.ShapeDtypeStruct((2, C, H // C, CZ), BF16),
         ),
         in_specs=[vmem, vmem, vmem, hbm, vmem, hbm],
         out_specs=(hbm,) * 4,
@@ -612,12 +588,17 @@
             pltpu.VMEM((NB, SQ, SL, CP * RB), BF16),
             pltpu.VMEM((C, GPB, CP, LANES), BF16),
             pltpu.VMEM((R * SQ, SL, CP * RB), BF16),
-            pltpu.VMEM((pieces_w, piece, CZ), BF16),
-            pltpu.VMEM((N - 1, piece, CZ), BF16),
-            pltpu.VMEM((pieces_w, piece, CZ), BF16),
-            pltpu.VMEM((pieces_v, 16, LANES), BF16),
-            pltpu.VMEM((N - 1, 16, LANES), BF16),
-            pltpu.VMEM((pieces_v, 16, LANES), BF16),
+            pltpu.VMEM((2, H, CZ), BF16),
+            pltpu.VMEM((H, CZ), BF16),
+            pltpu.VMEM((C, H // C, CZ), BF16),
+            pltpu.VMEM((C - 1, H // C, CZ), BF16),
+            pltpu.VMEM((NZ, H // C, CZ), BF16),
+            pltpu.VMEM((2, C, H // C, CZ), BF16),
+            pltpu.VMEM((2, CP, CM), BF16),
+            pltpu.VMEM((CP, CM), BF16),
+            pltpu.VMEM((C, CP, CM), BF16),
+            pltpu.VMEM((NZ, CP, CM), BF16),
+            pltpu.VMEM((2, CP, CM), BF16),
             dma((C,)),
             dma((NKB * SQ,)),
             dma((R * SQ,)),
@@ -626,8 +607,8 @@
             dma((C,)),
             dma((NB * SQ,)),
             dma((R * SQ,)),
-            dma((4,)),
-            dma((4,)),
+            dma((10,)),
+            dma((8,)),
         ],
         compiler_params=pltpu.CompilerParams(
             collective_id=0, has_side_effects=True, vmem_limit_bytes=56 * 1024 * 1024
@@ -650,9 +631,8 @@
             jax.ShapeDtypeStruct((CP, CM), F32),
             jax.ShapeDtypeStruct((CP * CP, CZ), F32),
         ),
-        in_specs=[hbm, hbm, vmem, vmem],
-        out_specs=(hbm, hbm, vmem, vmem, vmem),
-        scratch_shapes=[dma((2,))],
+        in_specs=[vmem] * 4,
+        out_specs=(vmem,) * 5,
         compiler_params=pltpu.CompilerParams(vmem_limit_bytes=56 * 1024 * 1024),
         name="finishing",
     )(pair, agrad, gv, gw)

time: 55.2 us -> 40.1 us (0.73)
  the two profiles are of different devices: /device:TPU:0 before, /device:TPU:1 now
where the time goes in v3:
time: 40.1 us; the launch traced here: 39.9 us
  Pallas kernels  39.3 us (98%)
  between operations  0.64 us (2%)
    pallas_call x1, Pallas kernels, body(): pl.pallas_call(functools.partial(kernel, dims), out_shape=(jax.ShapeDtype...  36.8 us
    pallas_call x1, Pallas kernels, body(): pl.pallas_call(finishing, out_shape=(jax.ShapeDtypeStruct(pair.shape, BF1...  2.43 us

profile of v3, /device:TPU:1, one launch (start us, length us, event | category | flops | bytes accessed | tf_op | source)
XLA Modules:
  0.0 39.9 jit_solution(6689814481975666020)
XLA Ops:
  0.6 36.8 %outer_product_mean.1 = (bf16[512,128]{1,0:T(8,128)(2,1)}, f32[256,256]{1,0:T(8,128)}, bf16[2,32,256]{2,1,0:T(8,128)(2,1)}, bf16[2,4,128,128]{3,2,1,0:T(8,128)(2,1)}) custom-call(bf16[256,256]{1,0:T(8,128)(2,1)} %bitcast.9, bf16[32,256]{1,0:T(8,128)(2,1)} %bitcast.11, bf16[32,256]{1,0:T(8,128)(2,1)} %bitcast.12, bf16[1024,128]{1,0:T(8,128)(2,1)} %wout_hbm.1, ...), custom_call_target="tpu_custom_call" | custom-call | tf_op jit(solution)/shard_map/outer_product_mean/pallas_call | solution.py:562
  37.5 2.4 %finishing.1 = (bf16[512,128]{1,0:T(8,128)(2,1)}, f32[256,256]{1,0:T(8,128)}, f32[32,256]{1,0:T(8,128)}, f32[32,256]{1,0:T(8,128)}, f32[1024,128]{1,0:T(8,128)}) custom-call(bf16[512,128]{1,0:T(8,128)(2,1)} %get-tuple-element.14.pair_in, f32[256,256]{1,0:T(8,128)} %get-tuple-element.15.agrad_in, bf16[2,32,256]{2,1,0:T(8,128)(2,1)} %get-tuple-element.16.gv_ref, ...), custom_call_target="tpu_custom_call" | custom-call | tf_op jit(solution)/shard_map/finishing/pallas_call | solution.py:625

commit v4 on v3

--- a/solution.py
+++ b/solution.py
@@ -45,17 +45,21 @@
 
 def kernel(
     dims,
-    align_ref,
-    lw_ref,
-    rw_ref,
+    align_hbm,
+    lw_hbm,
+    rw_hbm,
     wout_hbm,
-    bias_ref,
+    bias_hbm,
     cot_hbm,
     pair_hbm,
     agrad_hbm,
     gv_hbm,
     gw_hbm,
+    align_ref,
+    lw_ref,
+    rw_ref,
     wout_ref,
+    bias_ref,
     cot_ref,
     pair_ref,
     agrad_ref,
@@ -119,15 +123,24 @@
         return (div(lin, C * SQ), mod(div(lin, SQ), C), mod(lin, SQ))
 
     loads = [
-        pltpu.make_async_copy(wout_hbm, wout_ref, io_sem.at[0]),
-        pltpu.make_async_copy(cot_hbm, cot_ref, io_sem.at[1]),
+        pltpu.make_async_copy(src, dst, io_sem.at[k])
+        for k, (src, dst) in enumerate(
+            (
+                (align_hbm, align_ref),
+                (lw_hbm, lw_ref),
+                (rw_hbm, rw_ref),
+                (wout_hbm, wout_ref),
+                (cot_hbm, cot_ref),
+                (bias_hbm, bias_ref),
+            )
+        )
     ]
     for load in loads:
         load.start()
     stores = []
 
     def store(src, dst):
-        stores.append(pltpu.make_async_copy(src, dst, io_sem.at[2 + len(stores)]))
+        stores.append(pltpu.make_async_copy(src, dst, io_sem.at[len(loads) + len(stores)]))
         stores[-1].start()
 
     barrier = pltpu.get_barrier_semaphore()
@@ -138,6 +151,8 @@
 
     lax.fori_loop(1, N, greet, 0)
 
+    for load in loads[:3]:
+        load.wait()
     values = align_ref[...].astype(F32)
     center = values - jnp.mean(values, axis=1, keepdims=True)
     invstd = lax.rsqrt(jnp.mean(center * center, axis=1, keepdims=True) + 1e-05)
@@ -212,7 +227,7 @@
     def _():
         l3[s, pl.ds(l_slot * GPB, GPB)] = s_l[...]
 
-    for load in loads:
+    for load in loads[3:]:
         load.wait()
     wf[...] = wout_ref[...].astype(F32)
     for d in range(CP):
@@ -249,6 +264,43 @@
                     device_id_type=MESH,
                 ).wait_recv()
 
+    left = jnp.concatenate([l3[sq].reshape(G * CP, LANES) for sq in range(SQ)], axis=1)
+    eye_k = zero_one(iota((KS, KS), 0) == iota((KS, KS), 1))
+    left_turned = nt(eye_k, left).astype(BF16)
+    folded = []
+    for dh in range(DH):
+        z = nn(left_turned, og2[:, dh * CH : (dh + 1) * CH])
+        picked = []
+        for sq in range(SQ):
+            y = z[sq * I4 * SL : (sq * I4 + 1) * SL]
+            for i in range(1, I4):
+                start = (sq * I4 + i) * SL
+                y = jnp.where(i_lane == i, z[start : start + SL], y)
+            picked.append(y)
+        folded.append(nt(jnp.concatenate(picked, axis=0).astype(BF16), fold))
+    for b in range(NB):
+        for sq in range(SQ):
+            s_rg[b, sq] = jnp.concatenate(
+                [f[sq * SL : (sq + 1) * SL, b * PW : (b + 1) * PW] for f in folded], axis=1
+            ).astype(BF16)
+            owner = c * NB + b
+            here = jnp.logical_and(s == sq, blk == owner)
+
+            @pl.when(jnp.logical_not(here))
+            def _():
+                pltpu.make_async_remote_copy(
+                    src_ref=s_rg.at[b, sq],
+                    dst_ref=r_rg.at[my_t],
+                    send_sem=srg_sem.at[b * SQ + sq],
+                    recv_sem=rrg_sem.at[my_t],
+                    device_id=(owner // C, owner % C, sq),
+                    device_id_type=MESH,
+                ).start()
+
+            @pl.when(here)
+            def _():
+                r_rg[my_t] = s_rg[b, sq]
+
     for b in range(NB):
         for sq in range(SQ):
             away = jnp.logical_not(jnp.logical_and(s == sq, blk == c * NB + b))
@@ -264,7 +316,6 @@
                     device_id_type=MESH,
                 ).wait_recv()
 
-    left = jnp.concatenate([l3[sq].reshape(G * CP, LANES) for sq in range(SQ)], axis=1)
     for dh in range(DH):
         gathered = jnp.concatenate(
             [
@@ -283,6 +334,29 @@
                     i_lane == i, wide[sq * SL : (sq + 1) * SL], 0.0
                 ).astype(BF16)
 
+    lg = nt(og2[...], rbd[...]).astype(BF16)
+    for sq in range(SQ):
+        for g in range(G):
+            s_lg[sq, g] = lg[g * CP : (g + 1) * CP, sq * LANES : (sq + 1) * LANES]
+    for k in range(NKB):
+        for sq in range(SQ):
+            here = jnp.logical_and(s == sq, c == s * NKB + k)
+
+            @pl.when(jnp.logical_not(here))
+            def _():
+                pltpu.make_async_remote_copy(
+                    src_ref=s_lg.at[sq, pl.ds(k * GPB, GPB)],
+                    dst_ref=r_lg.at[c],
+                    send_sem=slg_sem.at[k * SQ + sq],
+                    recv_sem=rlg_sem.at[c],
+                    device_id=(r, s * NKB + k, sq),
+                    device_id_type=MESH,
+                ).start()
+
+            @pl.when(here)
+            def _():
+                r_lg[c] = s_lg[sq, pl.ds(k * GPB, GPB)]
+
     for dh in range(DH):
         part = nn(left, rbd[:, dh * CH : (dh + 1) * CH]) * inverse
         part = part.astype(BF16)
@@ -336,77 +410,10 @@
     s_w[...] = wo.astype(BF16).reshape(s_w.shape)
     send(s_w.at[1 - core], b_w, w_sem, 0, sibling)
 
-    eye_k = zero_one(iota((KS, KS), 0) == iota((KS, KS), 1))
-    left_turned = nt(eye_k, left).astype(BF16)
-    folded = []
-    for dh in range(DH):
-        z = nn(left_turned, og2[:, dh * CH : (dh + 1) * CH])
-        picked = []
-        for sq in range(SQ):
-            y = z[sq * I4 * SL : (sq * I4 + 1) * SL]
-            for i in range(1, I4):
-                start = (sq * I4 + i) * SL
-                y = jnp.where(i_lane == i, z[start : start + SL], y)
-            picked.append(y)
-        folded.append(nt(jnp.concatenate(picked, axis=0).astype(BF16), fold))
-    for b in range(NB):
-        for sq in range(SQ):
-            s_rg[b, sq] = jnp.concatenate(
-                [f[sq * SL : (sq + 1) * SL, b * PW : (b + 1) * PW] for f in folded], axis=1
-            ).astype(BF16)
-            owner = c * NB + b
-            here = jnp.logical_and(s == sq, blk == owner)
-
-            @pl.when(jnp.logical_not(here))
-            def _():
-                pltpu.make_async_remote_copy(
-                    src_ref=s_rg.at[b, sq],
-                    dst_ref=r_rg.at[my_t],
-                    send_sem=srg_sem.at[b * SQ + sq],
-                    recv_sem=rrg_sem.at[my_t],
-                    device_id=(owner // C, owner % C, sq),
-                    device_id_type=MESH,
-                ).start()
-
-            @pl.when(here)
-            def _():
-                r_rg[my_t] = s_rg[b, sq]
-
     drain(b_w, w_sem.at[1])
     p_w[...] = (s_w[core].astype(F32) + b_w[...].astype(F32)).astype(BF16).reshape(p_w.shape)
     for k in range(1, C):
         send(p_w.at[c ^ k], q_w.at[k - 1], w_sem, 1, (r, c ^ k, s))
-
-    lg = nt(og2[...], rbd[...]).astype(BF16)
-    for sq in range(SQ):
-        for g in range(G):
-            s_lg[sq, g] = lg[g * CP : (g + 1) * CP, sq * LANES : (sq + 1) * LANES]
-    for k in range(NKB):
-        for sq in range(SQ):
-            here = jnp.logical_and(s == sq, c == s * NKB + k)
-
-            @pl.when(jnp.logical_not(here))
-            def _():
-                pltpu.make_async_remote_copy(
-                    src_ref=s_lg.at[sq, pl.ds(k * GPB, GPB)],
-                    dst_ref=r_lg.at[c],
-                    send_sem=slg_sem.at[k * SQ + sq],
-                    recv_sem=rlg_sem.at[c],
-                    device_id=(r, s * NKB + k, sq),
-                    device_id_type=MESH,
-                ).start()
-
-            @pl.when(here)
-            def _():
-                r_lg[c] = s_lg[sq, pl.ds(k * GPB, GPB)]
-
-    pair_t = nn(w2_t, ot[...])
-    pair_ref[...] = (pair_t.T + bias_ref[...]).astype(BF16)
-    store(pair_ref, pair_hbm)
-
-    drain(q_w, w_sem.at[3])
-    z_w[zq] = (p_w[c].astype(F32) + total(q_w, C - 1)).astype(BF16)
-    send_line(z_w, w_sem, 2)
 
     for cc in range(C):
         here = jnp.logical_and(l_here, c == cc)
@@ -454,9 +461,9 @@
     s_v[1] = nn(gr_t, normed).astype(BF16)
     send(s_v.at[1 - core], b_v, v_sem, 0, sibling)
 
-    drain(z_w.at[pl.ds(0, NZ - 1)], w_sem.at[5])
-    f_w[core, c] = (total(z_w, NZ) * (1.0 / residues)).astype(BF16)
-    send_plane(f_w.at[core, c], f_w.at[core, c], w_sem, 3)
+    drain(q_w, w_sem.at[3])
+    z_w[zq] = (p_w[c].astype(F32) + total(q_w, C - 1)).astype(BF16)
+    send_line(z_w, w_sem, 2)
 
     drain(b_v, v_sem.at[1])
     p_v[c] = (s_v[core].astype(F32) + b_v[...].astype(F32)).astype(BF16)
@@ -475,12 +482,20 @@
     z_v[zq] = total(p_v, C).astype(BF16)
     send_line(z_v, v_sem, 2)
 
-    drain(f_w.at[0, pl.ds(0, C - 1)], w_sem.at[7])
-    send(f_w.at[core], f_w.at[core], w_sem, 4, sibling)
+    drain(z_w.at[pl.ds(0, NZ - 1)], w_sem.at[5])
+    f_w[core, c] = (total(z_w, NZ) * (1.0 / residues)).astype(BF16)
+    send_plane(f_w.at[core, c], f_w.at[core, c], w_sem, 3)
+
+    pair_t = nn(w2_t, ot[...])
+    pair_ref[...] = (pair_t.T + bias_ref[...]).astype(BF16)
+    store(pair_ref, pair_hbm)
 
     drain(z_v.at[pl.ds(0, NZ - 1)], v_sem.at[5])
     f_v[core] = (total(z_v, NZ) * (1.0 / residues)).astype(BF16)
     send(f_v.at[core], f_v.at[core], v_sem, 3, sibling)
+
+    drain(f_w.at[0, pl.ds(0, C - 1)], w_sem.at[7])
+    send(f_w.at[core], f_w.at[core], w_sem, 4, sibling)
 
     drain(f_w.at[0], w_sem.at[9])
     store(f_w, gw_hbm)
@@ -567,14 +582,18 @@
             jax.ShapeDtypeStruct((2, CP, CM), BF16),
             jax.ShapeDtypeStruct((2, C, H // C, CZ), BF16),
         ),
-        in_specs=[vmem, vmem, vmem, hbm, vmem, hbm],
+        in_specs=[hbm] * 6,
         out_specs=(hbm,) * 4,
         scratch_shapes=[
+            pltpu.VMEM((SL * RB, CM), BF16),
+            pltpu.VMEM((CP, CM), BF16),
+            pltpu.VMEM((CP, CM), BF16),
             pltpu.VMEM((CP * CP, CZ), BF16),
+            pltpu.VMEM((1, CZ), F32),
             pltpu.VMEM((rows * cols, CZ), BF16),
             pltpu.VMEM((rows * cols, CZ), BF16),
             pltpu.VMEM((SL * RB, CM), F32),
-            dma((6,)),
+            dma((10,)),
             pltpu.VMEM((GPB, CP, LANES), BF16),
             pltpu.VMEM((SL, CP * RB), BF16),
             pltpu.VMEM((SQ, G, CP, LANES), BF16),

time: 40.1 us -> 36 us (0.90)
  Pallas kernels: 39.3 us -> 35.2 us
    pallas_call x1, Pallas kernels: 36.8 us -> 32.8 us  [body(): pl.pallas_call(functools.partial(kernel, dims), out_shape=(jax.ShapeDtype...]
where the time goes in v4:
time: 36 us; the launch traced here: 35.9 us
  Pallas kernels  35.2 us (98%)
  between operations  0.64 us (2%)
    pallas_call x1, Pallas kernels, body(): pl.pallas_call(functools.partial(kernel, dims), out_shape=(jax.ShapeDtype...  32.8 us
    pallas_call x1, Pallas kernels, body(): pl.pallas_call(finishing, out_shape=(jax.ShapeDtypeStruct(pair.shape, BF1...  2.43 us

profile of v4, /device:TPU:1, one launch (start us, length us, event | category | flops | bytes accessed | tf_op | source)
XLA Modules:
  0.0 35.9 jit_solution(12277453398793087770)
XLA Ops:
  0.6 32.8 %outer_product_mean.1 = (bf16[512,128]{1,0:T(8,128)(2,1)}, f32[256,256]{1,0:T(8,128)}, bf16[2,32,256]{2,1,0:T(8,128)(2,1)}, bf16[2,4,128,128]{3,2,1,0:T(8,128)(2,1)}) custom-call(bf16[256,256]{1,0:T(8,128)(2,1)} %bitcast.9, bf16[32,256]{1,0:T(8,128)(2,1)} %bitcast.11, bf16[32,256]{1,0:T(8,128)(2,1)} %bitcast.12, bf16[1024,128]{1,0:T(8,128)(2,1)} %wout_hbm.1, ...), custom_call_target="tpu_custom_call" | custom-call | tf_op jit(solution)/shard_map/outer_product_mean/pallas_call | solution.py:577
  33.5 2.4 %finishing.1 = (bf16[512,128]{1,0:T(8,128)(2,1)}, f32[256,256]{1,0:T(8,128)}, f32[32,256]{1,0:T(8,128)}, f32[32,256]{1,0:T(8,128)}, f32[1024,128]{1,0:T(8,128)}) custom-call(bf16[512,128]{1,0:T(8,128)(2,1)} %get-tuple-element.14.pair_in, f32[256,256]{1,0:T(8,128)} %get-tuple-element.15.agrad_in, bf16[2,32,256]{2,1,0:T(8,128)(2,1)} %get-tuple-element.16.gv_ref, ...), custom_call_target="tpu_custom_call" | custom-call | tf_op jit(solution)/shard_map/finishing/pallas_call | solution.py:644

commit v5 on v4

--- a/solution.py
+++ b/solution.py
@@ -96,6 +96,7 @@
     rlg_sem,
     srg_sem,
     rrg_sem,
+    fw_sem,
     w_sem,
     v_sem,
 ):
@@ -118,6 +119,8 @@
     c = lax.axis_index("col")
     s = lax.axis_index("seq")
     me = (r * C + c) * SQ + s
+    core = mod(r, 2)
+    sibling = (r ^ 1, c, s)
 
     def dev(lin):
         return (div(lin, C * SQ), mod(div(lin, SQ), C), mod(lin, SQ))
@@ -207,6 +210,7 @@
     my_t = r * SQ + s
     for t in range(R * SQ):
         away = jnp.logical_not(jnp.logical_and(r_here, my_t == t))
+        away = jnp.logical_and(away, mod(r_slot, 2) == (t // SQ) % 2)
 
         @pl.when(away)
         def _():
@@ -264,6 +268,39 @@
                     device_id_type=MESH,
                 ).wait_recv()
 
+    def hand_over(b, sq):
+        return pltpu.make_async_remote_copy(
+            src_ref=r3.at[b, sq],
+            dst_ref=r3.at[b, sq],
+            send_sem=fw_sem.at[b * SQ + sq],
+            recv_sem=rr_sem.at[b * SQ + sq],
+            device_id=sibling,
+            device_id_type=MESH,
+        )
+
+    def from_sibling(b, sq):
+        return jnp.logical_and(s == sq, (r ^ 1) * C + c == c * NB + b)
+
+    def await_right(first):
+        for b in range(NB):
+            for sq in range(SQ):
+                mine = core == b % 2
+                if not first:
+                    mine = jnp.logical_not(mine)
+                own = jnp.logical_and(s == sq, blk == c * NB + b)
+
+                @pl.when(jnp.logical_and(mine, jnp.logical_not(own)))
+                def _():
+                    hand_over(b, sq).wait_recv()
+
+                if first:
+
+                    @pl.when(jnp.logical_and(mine, jnp.logical_not(from_sibling(b, sq))))
+                    def _():
+                        hand_over(b, sq).start()
+
+    await_right(True)
+
     left = jnp.concatenate([l3[sq].reshape(G * CP, LANES) for sq in range(SQ)], axis=1)
     eye_k = zero_one(iota((KS, KS), 0) == iota((KS, KS), 1))
     left_turned = nt(eye_k, left).astype(BF16)
@@ -301,20 +338,7 @@
             def _():
                 r_rg[my_t] = s_rg[b, sq]
 
-    for b in range(NB):
-        for sq in range(SQ):
-            away = jnp.logical_not(jnp.logical_and(s == sq, blk == c * NB + b))
-
-            @pl.when(away)
-            def _():
-                pltpu.make_async_remote_copy(
-                    src_ref=s_r,
-                    dst_ref=r3.at[b, sq],
-                    send_sem=sr_sem.at[0],
-                    recv_sem=rr_sem.at[b * SQ + sq],
-                    device_id=dev(me ^ 1),
-                    device_id_type=MESH,
-                ).wait_recv()
+    await_right(False)
 
     for dh in range(DH):
         gathered = jnp.concatenate(
@@ -367,8 +391,6 @@
                     g * CP : (g + 1) * CP, d * IJ : (d + 1) * IJ
                 ]
 
-    core = mod(r, 2)
-    sibling = (r ^ 1, c, s)
     NZ = R * SQ // 2
     zq = div(r, 2) * SQ + s
 
@@ -513,10 +535,19 @@
     drain(f_v.at[0], v_sem.at[6])
     for t in range(R * SQ):
         away = jnp.logical_not(jnp.logical_and(r_here, my_t == t))
+        away = jnp.logical_and(away, mod(r_slot, 2) == (t // SQ) % 2)
 
         @pl.when(away)
         def _():
             right_copy(t).wait_send()
+
+    for b in range(NB):
+        for sq in range(SQ):
+            gone = jnp.logical_and(core == b % 2, jnp.logical_not(from_sibling(b, sq)))
+
+            @pl.when(gone)
+            def _():
+                hand_over(b, sq).wait_send()
 
     for cc in range(C):
         away = jnp.logical_not(jnp.logical_and(l_here, c == cc))
@@ -626,6 +657,7 @@
             dma((C,)),
             dma((NB * SQ,)),
             dma((R * SQ,)),
+            dma((NB * SQ,)),
             dma((10,)),
             dma((8,)),
         ],

time: 36 us -> 36 us (level)
  no operation moved by 1% of the time
where the time goes in v5:
time: 36 us; the launch traced here: 35.9 us
  Pallas kernels  35.2 us (98%)
  between operations  0.64 us (2%)
    pallas_call x1, Pallas kernels, body(): pl.pallas_call(functools.partial(kernel, dims), out_shape=(jax.ShapeDtype...  32.8 us
    pallas_call x1, Pallas kernels, body(): pl.pallas_call(finishing, out_shape=(jax.ShapeDtypeStruct(pair.shape, BF1...  2.43 us

profile of v5, /device:TPU:1, one launch (start us, length us, event | category | flops | bytes accessed | tf_op | source)
XLA Modules:
  0.0 35.9 jit_solution(14705079703492015666)
XLA Ops:
  0.6 32.8 %outer_product_mean.1 = (bf16[512,128]{1,0:T(8,128)(2,1)}, f32[256,256]{1,0:T(8,128)}, bf16[2,32,256]{2,1,0:T(8,128)(2,1)}, bf16[2,4,128,128]{3,2,1,0:T(8,128)(2,1)}) custom-call(bf16[256,256]{1,0:T(8,128)(2,1)} %bitcast.9, bf16[32,256]{1,0:T(8,128)(2,1)} %bitcast.11, bf16[32,256]{1,0:T(8,128)(2,1)} %bitcast.12, bf16[1024,128]{1,0:T(8,128)(2,1)} %wout_hbm.1, ...), custom_call_target="tpu_custom_call" | custom-call | tf_op jit(solution)/shard_map/outer_product_mean/pallas_call | solution.py:608
  33.5 2.4 %finishing.1 = (bf16[512,128]{1,0:T(8,128)(2,1)}, f32[256,256]{1,0:T(8,128)}, f32[32,256]{1,0:T(8,128)}, f32[32,256]{1,0:T(8,128)}, f32[1024,128]{1,0:T(8,128)}) custom-call(bf16[512,128]{1,0:T(8,128)(2,1)} %get-tuple-element.14.pair_in, f32[256,256]{1,0:T(8,128)} %get-tuple-element.15.agrad_in, bf16[2,32,256]{2,1,0:T(8,128)(2,1)} %get-tuple-element.16.gv_ref, ...), custom_call_target="tpu_custom_call" | custom-call | tf_op jit(solution)/shard_map/finishing/pallas_call | solution.py:676

commit v6 on v4

--- a/solution.py
+++ b/solution.py
@@ -186,8 +186,8 @@
         return pltpu.make_async_remote_copy(
             src_ref=s_l,
             dst_ref=l3.at[s, pl.ds(l_slot * GPB, GPB)],
-            send_sem=sl_sem.at[cc],
-            recv_sem=rl_sem.at[l_slot * SQ + s],
+            send_sem=sl_sem.at[0],
+            recv_sem=rl_sem.at[0],
             device_id=(r, cc, l_tile),
             device_id_type=MESH,
         )
@@ -196,14 +196,27 @@
         return pltpu.make_async_remote_copy(
             src_ref=s_r,
             dst_ref=r3.at[r_slot, s],
-            send_sem=sr_sem.at[t],
-            recv_sem=rr_sem.at[r_slot * SQ + s],
+            send_sem=sr_sem.at[0],
+            recv_sem=rr_sem.at[0],
             device_id=(t // SQ, r_tile, t % SQ),
             device_id_type=MESH,
         )
 
     l_here = l_tile == s
     r_here = r_tile == c
+
+    def drain(ref, sem):
+        pltpu.make_async_copy(ref, ref, sem).wait()
+
+    def drain_blocks(count, sem, here):
+        @pl.when(here)
+        def _():
+            drain(r_rg.at[pl.ds(0, count - 1)], sem.at[0])
+
+        @pl.when(jnp.logical_not(here))
+        def _():
+            drain(r_rg.at[pl.ds(0, count)], sem.at[0])
+
     my_t = r * SQ + s
     for t in range(R * SQ):
         away = jnp.logical_not(jnp.logical_and(r_here, my_t == t))
@@ -249,20 +262,7 @@
     )
     i_lane = mod(div(iota((SL, CH), 1), cols), I4)
 
-    for k in range(NKB):
-        for sq in range(SQ):
-            away = jnp.logical_not(jnp.logical_and(s == sq, c == s * NKB + k))
-
-            @pl.when(away)
-            def _():
-                pltpu.make_async_remote_copy(
-                    src_ref=s_l,
-                    dst_ref=l3.at[sq, pl.ds(k * GPB, GPB)],
-                    send_sem=sl_sem.at[0],
-                    recv_sem=rl_sem.at[k * SQ + sq],
-                    device_id=dev(me ^ 1),
-                    device_id_type=MESH,
-                ).wait_recv()
+    drain_blocks(NKB * SQ, rl_sem, l_here)
 
     left = jnp.concatenate([l3[sq].reshape(G * CP, LANES) for sq in range(SQ)], axis=1)
     eye_k = zero_one(iota((KS, KS), 0) == iota((KS, KS), 1))
@@ -283,6 +283,8 @@
             s_rg[b, sq] = jnp.concatenate(
                 [f[sq * SL : (sq + 1) * SL, b * PW : (b + 1) * PW] for f in folded], axis=1
             ).astype(BF16)
+    for b in range(NB):
+        for sq in range(SQ):
             owner = c * NB + b
             here = jnp.logical_and(s == sq, blk == owner)
 
@@ -291,8 +293,8 @@
                 pltpu.make_async_remote_copy(
                     src_ref=s_rg.at[b, sq],
                     dst_ref=r_rg.at[my_t],
-                    send_sem=srg_sem.at[b * SQ + sq],
-                    recv_sem=rrg_sem.at[my_t],
+                    send_sem=srg_sem.at[0],
+                    recv_sem=rrg_sem.at[0],
                     device_id=(owner // C, owner % C, sq),
                     device_id_type=MESH,
                 ).start()
@@ -301,20 +303,7 @@
             def _():
                 r_rg[my_t] = s_rg[b, sq]
 
-    for b in range(NB):
-        for sq in range(SQ):
-            away = jnp.logical_not(jnp.logical_and(s == sq, blk == c * NB + b))
-
-            @pl.when(away)
-            def _():
-                pltpu.make_async_remote_copy(
-                    src_ref=s_r,
-                    dst_ref=r3.at[b, sq],
-                    send_sem=sr_sem.at[0],
-                    recv_sem=rr_sem.at[b * SQ + sq],
-                    device_id=dev(me ^ 1),
-                    device_id_type=MESH,
-                ).wait_recv()
+    drain_blocks(NB * SQ, rr_sem, r_here)
 
     for dh in range(DH):
         gathered = jnp.concatenate(
@@ -347,8 +336,8 @@
                 pltpu.make_async_remote_copy(
                     src_ref=s_lg.at[sq, pl.ds(k * GPB, GPB)],
                     dst_ref=r_lg.at[c],
-                    send_sem=slg_sem.at[k * SQ + sq],
-                    recv_sem=rlg_sem.at[c],
+                    send_sem=slg_sem.at[0],
+                    recv_sem=rlg_sem.at[0],
                     device_id=(r, s * NKB + k, sq),
                     device_id_type=MESH,
                 ).start()
@@ -397,9 +386,6 @@
                 (div(other, SQ) * 2 + core, c, mod(other, SQ)),
             )
 
-    def drain(ref, sem):
-        pltpu.make_async_copy(ref, ref, sem).wait()
-
     def total(ref, count):
         out = ref[0].astype(F32)
         for k in range(1, count):
@@ -415,33 +401,8 @@
     for k in range(1, C):
         send(p_w.at[c ^ k], q_w.at[k - 1], w_sem, 1, (r, c ^ k, s))
 
-    for cc in range(C):
-        here = jnp.logical_and(l_here, c == cc)
-
-        @pl.when(jnp.logical_not(here))
-        def _():
-            pltpu.make_async_remote_copy(
-                src_ref=s_l,
-                dst_ref=r_lg.at[cc],
-                send_sem=slg_sem.at[0],
-                recv_sem=rlg_sem.at[cc],
-                device_id=dev(me ^ 1),
-                device_id_type=MESH,
-            ).wait_recv()
-
-    for t in range(R * SQ):
-        here = jnp.logical_and(r_here, my_t == t)
-
-        @pl.when(jnp.logical_not(here))
-        def _():
-            pltpu.make_async_remote_copy(
-                src_ref=s_r,
-                dst_ref=r_rg.at[t],
-                send_sem=srg_sem.at[0],
-                recv_sem=rrg_sem.at[t],
-                device_id=dev(me ^ 1),
-                device_id_type=MESH,
-            ).wait_recv()
+    drain_blocks(C, rlg_sem, l_here)
+    drain_blocks(R * SQ, rrg_sem, r_here)
 
     gl = r_lg[0].astype(F32)
     for cc in range(1, C):
@@ -497,53 +458,25 @@
     drain(f_w.at[0, pl.ds(0, C - 1)], w_sem.at[7])
     send(f_w.at[core], f_w.at[core], w_sem, 4, sibling)
 
+    drain_blocks(C, sl_sem, l_here)
+    drain_blocks(R * SQ, sr_sem, r_here)
+    drain_blocks(NKB * SQ, slg_sem, l_here)
+    drain_blocks(NB * SQ, srg_sem, r_here)
+    drain(b_w, w_sem.at[0])
+    drain(q_w, w_sem.at[2])
+    drain(z_w.at[pl.ds(0, NZ - 1)], w_sem.at[4])
+    drain(f_w.at[0, pl.ds(0, C - 1)], w_sem.at[6])
+    drain(b_v, v_sem.at[0])
+    drain(p_v.at[pl.ds(0, C - 1)], v_sem.at[2])
+    drain(z_v.at[pl.ds(0, NZ - 1)], v_sem.at[4])
+
     drain(f_w.at[0], w_sem.at[9])
     store(f_w, gw_hbm)
     drain(f_v.at[0], v_sem.at[7])
     store(f_v, gv_hbm)
 
-    drain(b_w, w_sem.at[0])
-    drain(q_w, w_sem.at[2])
-    drain(z_w.at[pl.ds(0, NZ - 1)], w_sem.at[4])
-    drain(f_w.at[0, pl.ds(0, C - 1)], w_sem.at[6])
     drain(f_w.at[0], w_sem.at[8])
-    drain(b_v, v_sem.at[0])
-    drain(p_v.at[pl.ds(0, C - 1)], v_sem.at[2])
-    drain(z_v.at[pl.ds(0, NZ - 1)], v_sem.at[4])
     drain(f_v.at[0], v_sem.at[6])
-    for t in range(R * SQ):
-        away = jnp.logical_not(jnp.logical_and(r_here, my_t == t))
-
-        @pl.when(away)
-        def _():
-            right_copy(t).wait_send()
-
-    for cc in range(C):
-        away = jnp.logical_not(jnp.logical_and(l_here, c == cc))
-
-        @pl.when(away)
-        def _():
-            left_copy(cc).wait_send()
-
-    for b in range(NB):
-        for sq in range(SQ):
-            here = jnp.logical_and(s == sq, blk == c * NB + b)
-
-            @pl.when(jnp.logical_not(here))
-            def _():
-                pltpu.make_async_copy(
-                    s_rg.at[b, sq], s_rg.at[b, sq], srg_sem.at[b * SQ + sq]
-                ).wait()
-
-    for k in range(NKB):
-        for sq in range(SQ):
-            here = jnp.logical_and(s == sq, c == s * NKB + k)
-
-            @pl.when(jnp.logical_not(here))
-            def _():
-                part = s_lg.at[sq, pl.ds(k * GPB, GPB)]
-                pltpu.make_async_copy(part, part, slg_sem.at[k * SQ + sq]).wait()
-
     for copy in stores:
         copy.wait()
 
@@ -618,14 +551,14 @@
             pltpu.VMEM((C, CP, CM), BF16),
             pltpu.VMEM((NZ, CP, CM), BF16),
             pltpu.VMEM((2, CP, CM), BF16),
-            dma((C,)),
-            dma((NKB * SQ,)),
-            dma((R * SQ,)),
-            dma((NB * SQ,)),
-            dma((NKB * SQ,)),
-            dma((C,)),
-            dma((NB * SQ,)),
-            dma((R * SQ,)),
+            dma((1,)),
+            dma((1,)),
+            dma((1,)),
+            dma((1,)),
+            dma((1,)),
+            dma((1,)),
+            dma((1,)),
+            dma((1,)),
             dma((10,)),
             dma((8,)),
         ],

time: 36 us -> 35.8 us (level)
  no operation moved by 1% of the time
where the time goes in v6:
time: 35.8 us; the launch traced here: 35.6 us
  Pallas kernels  35 us (98%)
  between operations  0.64 us (2%)
    pallas_call x1, Pallas kernels, body(): pl.pallas_call(functools.partial(kernel, dims), out_shape=(jax.ShapeDtype...  32.6 us
    pallas_call x1, Pallas kernels, body(): pl.pallas_call(finishing, out_shape=(jax.ShapeDtypeStruct(pair.shape, BF1...  2.43 us

profile of v6, /device:TPU:1, one launch (start us, length us, event | category | flops | bytes accessed | tf_op | source)
XLA Modules:
  0.0 35.6 jit_solution(14448735452811878415)
XLA Ops:
  0.6 32.6 %outer_product_mean.1 = (bf16[512,128]{1,0:T(8,128)(2,1)}, f32[256,256]{1,0:T(8,128)}, bf16[2,32,256]{2,1,0:T(8,128)(2,1)}, bf16[2,4,128,128]{3,2,1,0:T(8,128)(2,1)}) custom-call(bf16[256,256]{1,0:T(8,128)(2,1)} %bitcast.9, bf16[32,256]{1,0:T(8,128)(2,1)} %bitcast.11, bf16[32,256]{1,0:T(8,128)(2,1)} %bitcast.12, bf16[1024,128]{1,0:T(8,128)(2,1)} %wout_hbm.1, ...), custom_call_target="tpu_custom_call" | custom-call | tf_op jit(solution)/shard_map/outer_product_mean/pallas_call | solution.py:510
  33.2 2.4 %finishing.1 = (bf16[512,128]{1,0:T(8,128)(2,1)}, f32[256,256]{1,0:T(8,128)}, f32[32,256]{1,0:T(8,128)}, f32[32,256]{1,0:T(8,128)}, f32[1024,128]{1,0:T(8,128)}) custom-call(bf16[512,128]{1,0:T(8,128)(2,1)} %get-tuple-element.14.pair_in, f32[256,256]{1,0:T(8,128)} %get-tuple-element.15.agrad_in, bf16[2,32,256]{2,1,0:T(8,128)(2,1)} %get-tuple-element.16.gv_ref, ...), custom_call_target="tpu_custom_call" | custom-call | tf_op jit(solution)/shard_map/finishing/pallas_call | solution.py:577

commit v7 on v6

--- a/solution.py
+++ b/solution.py
@@ -392,22 +392,27 @@
             out = out + ref[k].astype(F32)
         return out
 
-    wo = nn(ot[...], cot)
-    s_w[...] = wo.astype(BF16).reshape(s_w.shape)
+    H = s_w.shape[1]
+
+    def half(which):
+        start = pl.multiple_of(which * H, H)
+        s_w[which] = nn(ot[pl.ds(start, H), :], cot).astype(BF16)
+
+    half(1 - core)
     send(s_w.at[1 - core], b_w, w_sem, 0, sibling)
+    half(core)
+
+    pair_t = nn(w2_t, ot[...])
+    pair_ref[...] = (pair_t.T + bias_ref[...]).astype(BF16)
+    store(pair_ref, pair_hbm)
 
     drain(b_w, w_sem.at[1])
     p_w[...] = (s_w[core].astype(F32) + b_w[...].astype(F32)).astype(BF16).reshape(p_w.shape)
     for k in range(1, C):
         send(p_w.at[c ^ k], q_w.at[k - 1], w_sem, 1, (r, c ^ k, s))
 
-    drain_blocks(C, rlg_sem, l_here)
     drain_blocks(R * SQ, rrg_sem, r_here)
 
-    gl = r_lg[0].astype(F32)
-    for cc in range(1, C):
-        gl = gl + r_lg[cc].astype(F32)
-    gl = jnp.concatenate([gl[h] for h in range(GPB)], axis=1).astype(BF16)
     gr = r_rg[0].astype(F32)
     for t in range(1, R * SQ):
         gr = gr + r_rg[t].astype(F32)
@@ -418,8 +423,13 @@
         mod(iota((M, CP * RB), 0), RB) == mod(iota((M, CP * RB), 1), RB), gr_rows, 0.0
     ).astype(BF16)
     gr_t = nt(spread, gr_rows).astype(BF16)
+    s_v[1] = nn(gr_t, normed).astype(BF16)
+    drain_blocks(C, rlg_sem, l_here)
+    gl = r_lg[0].astype(F32)
+    for cc in range(1, C):
+        gl = gl + r_lg[cc].astype(F32)
+    gl = jnp.concatenate([gl[h] for h in range(GPB)], axis=1).astype(BF16)
     s_v[0] = nn(gl, normed_rs).astype(BF16)
-    s_v[1] = nn(gr_t, normed).astype(BF16)
     send(s_v.at[1 - core], b_v, v_sem, 0, sibling)
 
     drain(q_w, w_sem.at[3])
@@ -446,10 +456,6 @@
     drain(z_w.at[pl.ds(0, NZ - 1)], w_sem.at[5])
     f_w[core, c] = (total(z_w, NZ) * (1.0 / residues)).astype(BF16)
     send_plane(f_w.at[core, c], f_w.at[core, c], w_sem, 3)
-
-    pair_t = nn(w2_t, ot[...])
-    pair_ref[...] = (pair_t.T + bias_ref[...]).astype(BF16)
-    store(pair_ref, pair_hbm)
 
     drain(z_v.at[pl.ds(0, NZ - 1)], v_sem.at[5])
     f_v[core] = (total(z_v, NZ) * (1.0 / residues)).astype(BF16)

time: 35.8 us -> 36 us (level)
  no operation moved by 1% of the time
where the time goes in v7:
time: 36 us; the launch traced here: 35.8 us
  Pallas kernels  35.2 us (98%)
  between operations  0.64 us (2%)
    pallas_call x1, Pallas kernels, body(): pl.pallas_call(functools.partial(kernel, dims), out_shape=(jax.ShapeDtype...  32.7 us
    pallas_call x1, Pallas kernels, body(): pl.pallas_call(finishing, out_shape=(jax.ShapeDtypeStruct(pair.shape, BF1...  2.43 us

profile of v7, /device:TPU:1, one launch (start us, length us, event | category | flops | bytes accessed | tf_op | source)
XLA Modules:
  0.0 35.8 jit_solution(8389343678166605415)
XLA Ops:
  0.6 32.7 %outer_product_mean.1 = (bf16[512,128]{1,0:T(8,128)(2,1)}, f32[256,256]{1,0:T(8,128)}, bf16[2,32,256]{2,1,0:T(8,128)(2,1)}, bf16[2,4,128,128]{3,2,1,0:T(8,128)(2,1)}) custom-call(bf16[256,256]{1,0:T(8,128)(2,1)} %bitcast.9, bf16[32,256]{1,0:T(8,128)(2,1)} %bitcast.11, bf16[32,256]{1,0:T(8,128)(2,1)} %bitcast.12, bf16[1024,128]{1,0:T(8,128)(2,1)} %wout_hbm.1, ...), custom_call_target="tpu_custom_call" | custom-call | tf_op jit(solution)/shard_map/outer_product_mean/pallas_call | solution.py:516
  33.4 2.4 %finishing.1 = (bf16[512,128]{1,0:T(8,128)(2,1)}, f32[256,256]{1,0:T(8,128)}, f32[32,256]{1,0:T(8,128)}, f32[32,256]{1,0:T(8,128)}, f32[1024,128]{1,0:T(8,128)}) custom-call(bf16[512,128]{1,0:T(8,128)(2,1)} %get-tuple-element.14.pair_in, f32[256,256]{1,0:T(8,128)} %get-tuple-element.15.agrad_in, bf16[2,32,256]{2,1,0:T(8,128)(2,1)} %get-tuple-element.16.gv_ref, ...), custom_call_target="tpu_custom_call" | custom-call | tf_op jit(solution)/shard_map/finishing/pallas_call | solution.py:583
